TPU v7x, 128 devices: a whole 4x4x4 slice. The times are simulated.
128 devices in a mesh: ctx: 16 (over y_hi, z, core), tp: 8 (over x, y_lo).
Axes of the slice: x: 4, y: 4 (y_hi: 2, y_lo: 2; y = y_hi * 2 + y_lo), z: 4, core: 2. Of those that a mesh axis runs over, the one named last changes fastest.
Arguments:
- queries: bfloat16 [4096, 8192], P('ctx', 'tp'), may hold values from -160 to 160
- keys: bfloat16 [4096, 1024], P('ctx', 'tp'), may hold values from -6 to 6
- values: bfloat16 [4096, 1024], P('ctx', 'tp'), may hold values from -6 to 6
- dt_logits: bfloat16 [4096, 64], P('ctx', 'tp'), may hold values from -6 to 45056
- decay_log: float32 [64], P('tp'), may hold values from -13 to -3
- dt_bias: float32 [64], P('tp'), may hold values from -1 to 1
- c_weight: bfloat16 [64, 128, 128], P('tp'), may hold values from -0.5 to 0.5
- b_weight: bfloat16 [64, 128, 128], P('tp'), may hold values from -0.5 to 0.5
- x_weight: bfloat16 [64, 128, 128], P('tp'), may hold values from -0.5 to 0.5
- norm_gain: float32 [8192], P('tp'), may hold values from 0.5 to 1.5
Outputs:
- student_out: bfloat16 [4096, 8192], P('ctx', 'tp')
- grad_c: float32 [64, 128, 128], P('tp')
- grad_b: float32 [64, 128, 128], P('tp')
- grad_x: float32 [64, 128, 128], P('tp')
- grad_decay: float32 [64], P('tp')
- grad_bias: float32 [64], P('tp')
- grad_gain: float32 [8192], P('tp')
All inputs are finite; a program needn't handle non-finite values.
Results may differ from a plain program's by a relative error of at most 0.0023.
Values may be sent and summed in bfloat16 or wider, within the bound.
A program may use at most 128 MiB of HBM per device.

v0:
```python
import jax
import jax.numpy as jnp
from jax import lax
from jax.sharding import PartitionSpec as P

STRETCH = 256


epsilon = 1e-05
highest = lax.Precision.HIGHEST


def prefix(value, axis, join, neutral, backward):
    count, mine = (lax.axis_size(axis), lax.axis_index(axis))
    pieces = jax.tree.map(lambda part: lax.all_gather(part, axis), value)
    if backward:
        pieces = jax.tree.map(lambda part: part[::-1], pieces)
        mine = count - 1 - mine
    running = jax.tree.map(
        lambda part, zero: jnp.full_like(part, 0) + jnp.asarray(zero, part.dtype), value, neutral
    )

    def lap(position, running):
        longer = join(running, jax.tree.map(lambda part: part[position], pieces))
        return jax.tree.map(lambda new, old: jnp.where(position < mine, new, old), longer, running)

    return lax.fori_loop(0, count - 1, lap, running)


def project(q_heads, k_heads, v_heads, c_map, b_map, x_map):
    head_count = c_map.shape[0]
    kv_count = k_heads.shape[1]
    group_size = head_count // kv_count
    head_dim = c_map.shape[1]
    state_dim = c_map.shape[2]
    row_count = q_heads.shape[0]
    c_mat = jnp.einsum(
        "rhd,hdn->rhn", q_heads, c_map, preferred_element_type=jnp.float32
    ) * state_dim ** (-0.5)
    b_mat = jnp.einsum(
        "rkd,kgdn->rkgn",
        k_heads,
        b_map.reshape(kv_count, group_size, head_dim, state_dim),
        preferred_element_type=jnp.float32,
    )
    x_mat = jnp.einsum(
        "rkd,kgdp->rkgp",
        v_heads,
        x_map.reshape(kv_count, group_size, head_dim, head_dim),
        preferred_element_type=jnp.float32,
    )
    return (
        c_mat,
        b_mat.reshape(row_count, head_count, state_dim),
        x_mat.reshape(row_count, head_count, head_dim),
    )


def step_rates(dt_raw, decay_log, dt_bias):
    dt_step = jax.nn.softplus(dt_raw + dt_bias)
    log_keep = -jnp.exp(decay_log) * dt_step
    return (dt_step, log_keep)


def run_stretches(c_mat, b_mat, x_mat, dt_step, log_keep, state, stretch_len):
    row_count = c_mat.shape[0]
    stretch_count = row_count // stretch_len

    def split_rows(matrix):
        return matrix.reshape((stretch_count, stretch_len) + matrix.shape[1:])

    causal = jnp.arange(stretch_len)[:, None] >= jnp.arange(stretch_len)[None, :]

    def advance(carried, pieces):
        c_blk, b_blk, x_blk, dt_blk, keep_blk = pieces
        running = jnp.cumsum(keep_blk, axis=0)
        spans = running.T[:, :, None] - running.T[:, None, :]
        decay = (
            jnp.where(causal, jnp.exp(jnp.where(causal, spans, 0.0)), 0.0) * dt_blk.T[:, None, :]
        )
        scores = jnp.einsum("ihn,jhn->hij", c_blk, b_blk, precision=highest)
        inside = jnp.einsum("hij,jhp->ihp", scores * decay, x_blk, precision=highest)
        carried_in = jnp.einsum(
            "ihn,hnp->ihp", c_blk * jnp.exp(running)[:, :, None], carried, precision=highest
        )
        ending = running[-1]
        weights = jnp.exp(ending[None, :] - running) * dt_blk
        fresh = jnp.einsum("jhn,jhp->hnp", b_blk * weights[:, :, None], x_blk, precision=highest)
        return (jnp.exp(ending)[:, None, None] * carried + fresh, inside + carried_in)

    final_state, outputs = lax.scan(
        advance,
        state,
        (
            split_rows(c_mat),
            split_rows(b_mat),
            split_rows(x_mat),
            split_rows(dt_step),
            split_rows(log_keep),
        ),
    )
    return (outputs.reshape((row_count,) + outputs.shape[2:]), final_state)


def closing(b_mat, x_mat, dt_step, log_keep, state):
    running = jnp.cumsum(log_keep, axis=0)
    ending = running[-1]
    weights = jnp.exp(ending[None, :] - running) * dt_step
    spread = jnp.einsum("thn,thp->hnp", b_mat * weights[:, :, None], x_mat, precision=highest)
    return jnp.exp(ending)[:, None, None] * state + spread


def combine(earlier, later):
    return (earlier[0] * later[0], later[0][:, None, None] * earlier[1] + later[1])


def regroup(block, ctx_ways):
    return block.reshape((ctx_ways, block.shape[0] // ctx_ways, 1) + block.shape[1:])


def make_fold(q_group, q_place, key_place):
    row_count, kv_count, group_size, head_dim = q_group.shape
    scale = head_dim ** (-0.5)

    def fold(carried, piece, start):
        key_rows, value_rows = piece
        piece_rows = key_rows.shape[0]

        def update(block_index, current):
            best, row_total, accum = current
            first_row = block_index * row_count
            key_block = lax.dynamic_slice_in_dim(
                key_rows, block_index * row_count, row_count, 0
            ).reshape(row_count, kv_count, head_dim)
            value_block = lax.dynamic_slice_in_dim(
                value_rows, block_index * row_count, row_count, 0
            ).reshape(row_count, kv_count, head_dim)
            key_pos = key_place(first_row + jnp.arange(row_count, dtype=jnp.int32))
            scores = (
                jnp.einsum("lkgd,mkd->kglm", q_group, key_block, preferred_element_type=jnp.float32)
                * scale
            )
            scores = jnp.where(key_pos[None, :] <= q_place[:, None], scores, -1e30)
            raised = jnp.maximum(best, jnp.max(scores, axis=3))
            weights = jnp.exp(scores - raised[..., None])
            shrink = jnp.exp(best - raised)
            row_total = row_total * shrink + jnp.sum(weights, axis=3)
            mixed = jnp.einsum(
                "kglm,mkd->lkgd", weights, value_block.astype(jnp.float32), precision=highest
            )
            accum = accum * jnp.transpose(shrink, (2, 0, 1))[..., None] + mixed
            return (raised, row_total, accum)

        def visit(block_index, current):
            return update(block_index, current)

        return lax.fori_loop(0, piece_rows // row_count, visit, carried)

    return fold


def finish(row_total, accum):
    row_count = accum.shape[0]
    return (
        (accum / jnp.transpose(row_total, (2, 0, 1))[..., None])
        .reshape(row_count, -1)
        .astype(jnp.bfloat16)
    )


def local(
    queries, keys, values, dt_logits, decay_log, dt_bias, c_weight, b_weight, x_weight, norm_gain
):
    row_count = queries.shape[0]
    ctx_ways = lax.axis_size("ctx")
    ctx_rank = lax.axis_index("ctx")
    head_count = decay_log.shape[0]
    head_dim = c_weight.shape[1]
    state_dim = c_weight.shape[2]
    kv_count = keys.shape[1] // head_dim
    group_size = head_count // kv_count
    features = head_count * head_dim * lax.axis_size("tp")
    total_tokens = row_count * ctx_ways
    moved = (
        lax.all_to_all(regroup(queries, ctx_ways), "ctx", split_axis=0, concat_axis=2, tiled=True),
        lax.all_to_all(regroup(keys, ctx_ways), "ctx", split_axis=0, concat_axis=2, tiled=True),
        lax.all_to_all(regroup(values, ctx_ways), "ctx", split_axis=0, concat_axis=2, tiled=True),
        lax.all_to_all(
            regroup(dt_logits, ctx_ways), "ctx", split_axis=0, concat_axis=2, tiled=True
        ),
    )
    q_rows, k_rows, v_rows, z_rows = [member.reshape(row_count, -1) for member in moved]
    start_carry = (
        jnp.full((kv_count, group_size, row_count), -1e30, jnp.float32),
        jnp.zeros((kv_count, group_size, row_count), jnp.float32),
        jnp.zeros((row_count, kv_count, group_size, head_dim), jnp.float32),
    )
    positions = jnp.arange(row_count, dtype=jnp.int32)
    q_group = queries.reshape(row_count, kv_count, group_size, head_dim)

    def given_place(index):
        return index % row_count * ctx_ways + index // row_count

    folding = make_fold(q_group, positions * ctx_ways + ctx_rank, given_place)
    unused_best, row_total, accum = folding(
        start_carry,
        (
            lax.all_gather(keys, "ctx", axis=0, tiled=True),
            lax.all_gather(values, "ctx", axis=0, tiled=True),
        ),
        jnp.int32(0),
    )
    given_out = finish(row_total, accum)
    teacher_out = lax.all_to_all(
        regroup(given_out, ctx_ways), "ctx", split_axis=0, concat_axis=2, tiled=True
    ).reshape(row_count, -1)
    q_heads = q_rows.reshape(row_count, head_count, head_dim)
    k_heads = k_rows.reshape(row_count, kv_count, head_dim)
    v_heads = v_rows.reshape(row_count, kv_count, head_dim)
    z_feats = z_rows.astype(jnp.float32)
    c_mat, b_mat, x_mat = project(q_heads, k_heads, v_heads, c_weight, b_weight, x_weight)

    def rates_only(log_rate, bias_vec):
        return step_rates(z_feats, log_rate, bias_vec)

    rate_pair, undo_rates = jax.vjp(rates_only, decay_log, dt_bias)
    dt_step, log_keep = rate_pair
    empty_state = jnp.zeros((head_count, state_dim, head_dim), jnp.float32)
    own_state = closing(b_mat, x_mat, dt_step, log_keep, empty_state)
    fading = jnp.exp(jnp.sum(log_keep, axis=0))
    identity = (jnp.ones_like(fading), jnp.zeros_like(own_state))
    incoming = prefix((fading, own_state), "ctx", combine, identity, False)[1]

    def mixing(c_in, b_in, x_in, dt_in, keep_in, state_in):
        return run_stretches(c_in, b_in, x_in, dt_in, keep_in, state_in, STRETCH)[0]

    mixed, undo_mix = jax.vjp(mixing, c_mat, b_mat, x_mat, dt_step, log_keep, incoming)
    flat = mixed.reshape(row_count, head_count * head_dim)
    teacher_flat = teacher_out.astype(jnp.float32)
    squares, teacher_squares = lax.psum(
        (jnp.sum(flat * flat, axis=1), jnp.sum(teacher_flat * teacher_flat, axis=1)), "tp"
    )
    inverse = lax.rsqrt(squares / features + epsilon)
    target = teacher_flat * lax.rsqrt(teacher_squares / features + epsilon)[:, None]
    normed = flat * inverse[:, None] * norm_gain
    student_out = normed.astype(jnp.bfloat16)
    d_normed = 2.0 * (normed - target) / total_tokens
    grad_gain_local = jnp.sum(d_normed * flat * inverse[:, None], axis=0)
    weighted = d_normed * norm_gain
    cross = lax.psum(jnp.sum(weighted * flat, axis=1), "tp")
    d_flat = (
        weighted * inverse[:, None]
        - flat * (inverse * inverse * inverse * cross / features)[:, None]
    )
    d_c, d_b, d_x, d_step, d_keep, d_state = undo_mix(
        d_flat.reshape(row_count, head_count, head_dim)
    )
    leaving = prefix((fading, d_state), "ctx", combine, identity, True)[1]
    unused_out, undo_close = jax.vjp(closing, b_mat, x_mat, dt_step, log_keep, incoming)
    e_b, e_x, e_step, e_keep, unused_state = undo_close(leaving)
    b_total = (d_b + e_b).reshape(row_count, kv_count, group_size, state_dim)
    x_total = (d_x + e_x).reshape(row_count, kv_count, group_size, head_dim)
    g_c = jnp.einsum(
        "rhd,rhn->hdn", q_heads.astype(jnp.float32), d_c, precision=highest
    ) * state_dim ** (-0.5)
    g_b = jnp.einsum(
        "rkd,rkgn->kgdn", k_heads.astype(jnp.float32), b_total, precision=highest
    ).reshape(head_count, head_dim, state_dim)
    g_x = jnp.einsum(
        "rkd,rkgp->kgdp", v_heads.astype(jnp.float32), x_total, precision=highest
    ).reshape(head_count, head_dim, head_dim)
    g_decay, g_bias = undo_rates((d_step + e_step, d_keep + e_keep))
    summed = lax.psum((g_c, g_b, g_x, g_decay, g_bias, grad_gain_local), "ctx")
    return (student_out, summed[0], summed[1], summed[2], summed[3], summed[4], summed[5])


def solution(mesh):
    return jax.shard_map(
        local,
        mesh=mesh,
        in_specs=(
            P("ctx", "tp"),
            P("ctx", "tp"),
            P("ctx", "tp"),
            P("ctx", "tp"),
            P("tp"),
            P("tp"),
            P("tp", None, None),
            P("tp", None, None),
            P("tp", None, None),
            P("tp"),
        ),
        out_specs=(
            P("ctx", "tp"),
            P("tp", None, None),
            P("tp", None, None),
            P("tp", None, None),
            P("tp"),
            P("tp"),
            P("tp"),
        ),
        check_vma=False,
    )
```

profile of v0, /device:TPU:1, one launch (start us, length us, event | category | flops | bytes accessed | tf_op | source)
XLA Modules:
  0.0 540.3 jit_solution(12402442889197580161)
XLA Ops:
  10.3 9.5 %all-to-all-start.2 = ((bf16[16,16,1,8]{1,3,2,0:T(8,128)(2,1)}), bf16[16,16,1,8]{1,3,2,0:T(8,128)(2,1)S(1)}, u32[]{:S(2)}, u32[]{:S(2)}) async-start(bf16[16,16,1,8]{1,3,2,0:T(8,128)(2,1)} %copy.176), calls=%async_computation.2 | async-start | bytes 65536 | tf_op jit(solution)/shard_map/all_to_all | solution.py:188
  27.1 6.4 %all-to-all-start.1 = ((bf16[16,16,1,128]{3,1,2,0:T(8,128)(2,1)}), bf16[16,16,1,128]{3,1,2,0:T(8,128)(2,1)S(1)}, u32[]{:S(2)}, u32[]{:S(2)}) async-start(bf16[16,16,1,128]{3,1,2,0:T(8,128)(2,1)} %bitcast.4), calls=%async_computation.1 | async-start | bytes 131072 | tf_op jit(solution)/shard_map/all_to_all | solution.py:186
  36.4 4.4 all-to-all-done.1
  40.8 3.7 all-to-all-start.3
  44.6 33.0 %all-reduce.2 = f32[128]{0:T(128)S(1)} all-reduce(f32[128]{0:T(128)S(1)} %exponential_dynamic-update-slice_fusion), channel_id=2, replica_groups=mesh['ctx'=16,'tp'=8] {'ctx'}, use_global_device_ids=true, to_apply=%add.2 | all-reduce | flops 128 | bytes 1024
  78.4 8.9 %all-to-all-start = ((bf16[16,16,1,1024]{3,1,2,0:T(8,128)(2,1)}), bf16[16,16,1,1024]{3,1,2,0:T(8,128)(2,1)S(1)}, u32[]{:S(2)}, u32[]{:S(2)}) async-start(bf16[16,16,1,1024]{3,1,2,0:T(8,128)(2,1)} %bitcast), calls=%async_computation | async-start | bytes 1048576 | tf_op jit(solution)/shard_map/all_to_all | solution.py:185
  91.1 10.4 %all-to-all-done = bf16[16,16,1,1024]{3,1,2,0:T(8,128)(2,1)S(1)} async-done(((bf16[16,16,1,1024]{3,1,2,0:T(8,128)(2,1)}), bf16[16,16,1,1024]{3,1,2,0:T(8,128)(2,1)S(1)}, u32[]{:S(2)}, u32[]{:S(2)}) %all-to-all-start) | async-done | bytes 524320 | tf_op jit(solution)/shard_map/all_to_all | solution.py:185
  106.9 87.4 %while.35 = (s32[]{:T(128)}, f32[1,8,256]{2,1,0:T(8,128)S(1)}, f32[1,8,256]{2,1,0:T(8,128)S(1)}, f32[256,1,8,128]{0,3,2,1:T(8,128)}, bf16[4096,128]{1,0:T(8,128)...) while((s32[]{:T(128)}, f32[1,8,256]{2,1,0:T(8,128)S(1)}, ...), condition=%wide.region_10.11_spmd.clone, body=%wide.region_7.10_spmd.clone.sunk | while | flops 943540224 | bytes 9310399 | solution.py:157
  113.7 3.4 fusion.164
  119.2 3.5 fusion.164
  124.8 3.4 fusion.164
  130.3 3.4 fusion.164
  135.7 3.4 fusion.164
  141.2 3.4 fusion.164
  152.2 3.4 fusion.164
  163.1 3.4 fusion.164
  174.1 3.4 fusion.164
  179.6 3.4 fusion.164
  190.5 3.4 fusion.164
  197.1 4.1 all-to-all-start.4
  205.0 4.0 fusion.33
  209.0 3.5 all-to-all-done.4
  217.2 18.2 %while.34 = (s32[]{:T(128)}, f32[8,128,128]{2,1,0:T(8,128)S(1)}, s32[]{:T(128)}, f32[16,8]{1,0:T(8,128)S(1)}, f32[16,8,128,128]{3,2,1,0:T(8,128)}, /*index=5*/s32[]{:T(128)}, s32[]{:T(128)}) while((s32[]{:T(128)}, f32[8,128,128]{2,1,0:T(8,128)S(1)}, s32[]{:T(128)}, f32[16,8]{1,0:T(8,128)S(1)}, f32[16,8,128,128]{3,2,1,0:T(8,128)}, ...), condition=%wide.region_4.5_spmd.clone, body=%wide.region_3.4_spmd.clone.sunk | while | flops 524292 | bytes 1573065 | solution.py:27
  235.5 3.4 fusion.49
  238.9 15.6 %all-reduce.5 = (f32[256]{0:T(256)S(1)}, f32[256]{0:T(256)S(1)}) all-reduce(f32[256]{0:T(256)S(1)} %get-tuple-element.911, f32[256]{0:T(256)S(1)} %reduce_sum.249), channel_id=1, replica_groups=mesh['ctx'=16,'tp'=8] {'tp'}, use_global_device_ids=true, to_apply=%region_6.7 | all-reduce | flops 512 | bytes 4096 | tf_op jit(solution)/shard_map/psum | solution.py:240
  257.3 12.5 %psum.65 = f32[256]{0:T(256)S(1)} all-reduce(f32[256]{0:T(256)S(1)} %get-tuple-element.841), channel_id=1, replica_groups=mesh['ctx'=16,'tp'=8] {'tp'}, use_global_device_ids=true, to_apply=%region_14.15 | all-reduce | flops 256 | bytes 2048 | tf_op jit(solution)/shard_map/psum | solution.py:250
  283.6 4.0 fusion.39
  295.0 56.9 %all-gather.14.cloned.1.call-done = f32[128,128,128]{2,1,0:T(8,128)} async-done(((f32[8,128,128]{2,1,0:T(8,128)}), f32[128,128,128]{2,1,0:T(8,128)}) %all-gather.14.cloned.1.call-update) | async-done | bytes 8388624 | tf_op jit(solution)/shard_map/all_gather | solution.py:15
  351.9 7.7 %rev.7 = f32[16,8,128,128]{3,2,1,0:T(8,128)} reverse(f32[16,8,128,128]{3,2,1,0:T(8,128)} %bitcast.323), dimensions={0} | reverse | bytes 16777216 | tf_op jit(solution)/shard_map/rev | solution.py:17
  359.6 18.4 %while.36 = (s32[]{:T(128)}, f32[8,128,128]{2,1,0:T(8,128)S(1)}, s32[]{:T(128)}, f32[16,8]{1,0:T(8,128)S(1)}, f32[16,8,128,128]{3,2,1,0:T(8,128)}, /*index=5*/s32[]{:T(128)}, s32[]{:T(128)}) while((s32[]{:T(128)}, f32[8,128,128]{2,1,0:T(8,128)S(1)}, s32[]{:T(128)}, f32[16,8]{1,0:T(8,128)S(1)}, f32[16,8,128,128]{3,2,1,0:T(8,128)}, ...), condition=%wide.region_17.18_spmd.clone, body=%wide.region_16.17_spmd.clone.sunk | while | flops 524292 | bytes 1573065 | solution.py:27
  395.0 34.1 %all-reduce.3 = (f32[8]{0:T(128)}, f32[8]{0:T(128)}, f32[1024]{0:T(1024)}) all-reduce(f32[8]{0:T(128)S(1)} %negate_multiply_fusion, f32[8]{0:T(128)S(1)} %get-tuple-element.846, f32[1024]{0:T(1024)S(1)} %bitcast.344), channel_id=1, replica_groups=mesh['ctx'=16,'tp'=8] {'ctx'}, use_global_device_ids=true, to_apply=%region_34.35 | all-reduce | flops 1040 | bytes 8320 | tf_op jit(solution)/shard_map/psum | solution.py:273
  429.1 99.3 %all-reduce.8.cloned.1.call-done = (f32[8,128,128]{1,2,0:T(8,128)}, f32[8,128,128]{1,2,0:T(8,128)}, f32[8,128,128]{1,2,0:T(8,128)}) async-done(((f32[8,128,128]{1,2,0:T(8,128)}, f32[8,128,128]{1,2,0:T(8,128)}, f32[8,128,128]{1,2,0:T(8,128)}), (f32[8,128,128]{1,2,0:T(8,128)}, f32[8,128,128]{1,2,0:T(8,128)}, f32[8,128,128]{1,2,0:T(8,128)})) %all-reduce.8.cloned.1.call-update) | async-done | bytes 1572880 | tf_op jit(solution)/shard_map/psum | solution.py:273
  (391 shorter events, 163.6 us)
Async XLA Ops:
  7.2 80.2 %copy-start = (bf16[8,128,128]{2,1,0:T(8,128)(2,1)S(1)}, bf16[8,128,128]{2,1,0:T(8,128)(2,1)}, u32[]{:S(2)}) copy-start(bf16[8,128,128]{2,1,0:T(8,128)(2,1)} %param.23) | copy-start | bytes 786436
  7.2 17.6 %copy-start.53 = (u32[128]{0:T(128)S(1)}, u32[128]{0:T(128)}, u32[]{:S(2)}) copy-start(u32[128]{0:T(128)} %constant.326) | copy-start | bytes 1540
  7.2 26.4 %copy-start.41 = (f32[8]{0:T(128)S(1)}, f32[8]{0:T(128)}, u32[]{:S(2)}) copy-start(f32[8]{0:T(128)} %param.21) | copy-start | bytes 100
  7.2 96.8 %all-gather.10.cloned.1.call-start = ((), (), s32[]{:S(2)}) async-start(), calls=%async_computation.6 | async-start | bytes 1114112 | tf_op jit(solution)/shard_map/all_gather | solution.py:209
  10.3 16.8 %all-to-all-start.2 = ((bf16[16,16,1,8]{1,3,2,0:T(8,128)(2,1)}), bf16[16,16,1,8]{1,3,2,0:T(8,128)(2,1)S(1)}, u32[]{:S(2)}, u32[]{:S(2)}) async-start(bf16[16,16,1,8]{1,3,2,0:T(8,128)(2,1)} %copy.176), calls=%async_computation.2 | async-start | bytes 65536 | tf_op jit(solution)/shard_map/all_to_all | solution.py:188
  19.8 87.2 %all-gather.8.cloned.1.call-start = ((), (), s32[]{:S(2)}) async-start(), calls=%async_computation.5 | async-start | bytes 1114112 | tf_op jit(solution)/shard_map/all_gather | solution.py:208
  21.2 66.2 %copy-start.48 = (f32[8]{0:T(128)}, f32[8]{0:T(128)S(1)}, u32[]{:S(2)}) copy-start(f32[8]{0:T(128)S(1)} %exponential_negate_fusion) | copy-start | bytes 100
  23.8 64.0 %copy-start.25 = (bf16[8,128,128]{2,1,0:T(8,128)(2,1)S(1)}, bf16[8,128,128]{2,1,0:T(8,128)(2,1)}, u32[]{:S(2)}) copy-start(bf16[8,128,128]{2,1,0:T(8,128)(2,1)} %param.24) | copy-start | bytes 786436
  27.1 13.7 %all-to-all-start.1 = ((bf16[16,16,1,128]{3,1,2,0:T(8,128)(2,1)}), bf16[16,16,1,128]{3,1,2,0:T(8,128)(2,1)S(1)}, u32[]{:S(2)}, u32[]{:S(2)}) async-start(bf16[16,16,1,128]{3,1,2,0:T(8,128)(2,1)} %bitcast.4), calls=%async_computation.1 | async-start | bytes 131072 | tf_op jit(solution)/shard_map/all_to_all | solution.py:186
  33.6 44.7 %copy-start.28 = (f32[256,8]{0,1:T(8,128)}, f32[256,8]{0,1:T(8,128)S(1)}, u32[]{:S(2)}) copy-start(f32[256,8]{0,1:T(8,128)S(1)} %reshape.668) | copy-start | bytes 24580
  35.2 43.1 %copy-start.22 = (f32[256,8]{0,1:T(8,128)}, f32[256,8]{0,1:T(8,128)S(1)}, u32[]{:S(2)}) copy-start(f32[256,8]{0,1:T(8,128)S(1)} %get-tuple-element.899) | copy-start | bytes 24580
  35.4 5.4 copy-start.43
  35.4 52.7 %copy-start.50 = (f32[8]{0:T(128)}, f32[8]{0:T(128)S(1)}, u32[]{:S(2)}) copy-start(f32[8]{0:T(128)S(1)} %exponential_multiply_fusion) | copy-start | bytes 100
  36.2 52.0 %copy-start.26 = (f32[256,8]{0,1:T(8,128)}, f32[256,8]{0,1:T(8,128)S(1)}, u32[]{:S(2)}) copy-start(f32[256,8]{0,1:T(8,128)S(1)} %get-tuple-element.906) | copy-start | bytes 24580
  40.8 37.6 %all-to-all-start.3 = ((bf16[16,16,1,128]{3,1,2,0:T(8,128)(2,1)}), bf16[16,16,1,128]{3,1,2,0:T(8,128)(2,1)S(1)}, u32[]{:S(2)}, u32[]{:S(2)}) async-start(bf16[16,16,1,128]{3,1,2,0:T(8,128)(2,1)} %bitcast.18), calls=%async_computation.3 | async-start | bytes 131072 | tf_op jit(solution)/shard_map/all_to_all | solution.py:187
  78.4 23.1 %all-to-all-start = ((bf16[16,16,1,1024]{3,1,2,0:T(8,128)(2,1)}), bf16[16,16,1,1024]{3,1,2,0:T(8,128)(2,1)S(1)}, u32[]{:S(2)}, u32[]{:S(2)}) async-start(bf16[16,16,1,1024]{3,1,2,0:T(8,128)(2,1)} %bitcast), calls=%async_computation | async-start | bytes 1048576 | tf_op jit(solution)/shard_map/all_to_all | solution.py:185
  87.3 129.9 %all-gather.12.cloned.1.call-start = ((), (), s32[]{:S(2)}) async-start(), calls=%async_computation.7 | async-start | bytes 8912896 | tf_op jit(solution)/shard_map/all_gather | solution.py:15
  89.1 13.6 %copy-start.24 = (bf16[8,128,128]{2,1,0:T(8,128)(2,1)S(1)}, bf16[8,128,128]{2,1,0:T(8,128)(2,1)}, u32[]{:S(2)}) copy-start(bf16[8,128,128]{2,1,0:T(8,128)(2,1)} %param.22) | copy-start | bytes 786436
  91.0 15.9 %copy-start.21 = (f32[1,8,256]{2,1,0:T(8,128)S(1)}, f32[1,8,256]{2,1,0:T(8,128)}, u32[]{:S(2)}) copy-start(f32[1,8,256]{2,1,0:T(8,128)} %custom-call.2) | copy-start | bytes 24580
  194.3 7.4 %copy-start.2 = (f32[256,8,128]{0,2,1:T(8,128)S(1)}, f32[256,8,128]{0,2,1:T(8,128)}, u32[]{:S(2)}) copy-start(f32[256,8,128]{0,2,1:T(8,128)} %convolution_bitcast_fusion.4) | copy-start | bytes 3145732
  197.1 15.4 %all-to-all-start.4 = ((bf16[16,16,1,1024]{3,1,2,0:T(8,128)(2,1)}), bf16[16,16,1,1024]{3,1,2,0:T(8,128)(2,1)S(1)}, u32[]{:S(2)}, u32[]{:S(2)}) async-start(bf16[16,16,1,1024]{3,1,2,0:T(8,128)(2,1)} %bitcast.42), calls=%async_computation.4 | async-start | bytes 1048576 | tf_op jit(solution)/shard_map/all_to_all | solution.py:214
  201.1 150.8 %all-gather.14.cloned.1.call-start = ((), (), s32[]{:S(2)}) async-start(), calls=%async_computation.8 | async-start | bytes 8912896 | tf_op jit(solution)/shard_map/all_gather | solution.py:15
  217.2 18.2 %copy-start.32 = (f32[256,8]{0,1:T(8,128)S(1)}, f32[256,8]{0,1:T(8,128)}, u32[]{:S(2)}) copy-start(f32[256,8]{0,1:T(8,128)} %get-tuple-element.910) | copy-start | bytes 24580
  235.5 19.0 %copy-start.35 = (f32[1024]{0:T(1024)S(1)}, f32[1024]{0:T(1024)}, u32[]{:S(2)}) copy-start(f32[1024]{0:T(1024)} %param.25) | copy-start | bytes 12292
  235.5 19.0 %copy-start.36 = (f32[8,128]{1,0:T(8,128)S(1)}, f32[8,128]{1,0:T(8,128)}, u32[]{:S(2)}) copy-start(f32[8,128]{1,0:T(8,128)} %multiply_bitcast_fusion.1) | copy-start | bytes 12292
  257.3 15.4 %copy-start.51 = (f32[8]{0:T(128)S(1)}, f32[8]{0:T(128)}, u32[]{:S(2)}) copy-start(f32[8]{0:T(128)} %copy-done.50) | copy-start | bytes 100
  274.6 253.8 %all-reduce.8.cloned.1.call-start = ((), (), s32[]{:S(2)}) async-start(), calls=%async_computation.9 | async-start | bytes 3145728 | tf_op jit(solution)/shard_map/psum | solution.py:273
  387.0 7.8 %copy-start.45 = (f32[8,256]{1,0:T(8,128)S(1)}, f32[8,256]{1,0:T(8,128)}, u32[]{:S(2)}) copy-start(f32[8,256]{1,0:T(8,128)} %get-tuple-element.839) | copy-start | bytes 24580
  387.0 7.8 %copy-start.49 = (f32[8]{0:T(128)S(1)}, f32[8]{0:T(128)}, u32[]{:S(2)}) copy-start(f32[8]{0:T(128)} %copy-done.48) | copy-start | bytes 100
  387.0 8.0 %copy-start.52 = (f32[8]{0:T(128)S(1)}, f32[8]{0:T(128)}, u32[]{:S(2)}) copy-start(f32[8]{0:T(128)} %param.20) | copy-start | bytes 100
  387.0 8.0 %copy-start.40 = (f32[8,128]{1,0:T(8,128)S(1)}, f32[8,128]{1,0:T(8,128)}, u32[]{:S(2)}) copy-start(f32[8,128]{1,0:T(8,128)} %get-tuple-element.840) | copy-start | bytes 12292
  388.9 144.7 %copy-start.1 = (bf16[8,128,128]{2,1,0:T(8,128)(2,1)S(1)}, bf16[8,128,128]{2,1,0:T(8,128)(2,1)}, u32[]{:S(2)}) copy-start(bf16[8,128,128]{2,1,0:T(8,128)(2,1)} %param.23) | copy-start | bytes 786436
  (32 other events, 72.9 us)
Sparse Core Ops, SparseCore 0:
  10.9 47.2 all-gather.9
  60.7 46.1 all-gather.7
  110.0 71.6 all-gather.11
  274.8 77.0 all-gather.13
  388.6 139.7 all-reduce.7
where the time goes:
time: 550 us; the launch traced here: 540 us
  waiting for transfers between devices  179 us (33%)
  matrix products  120 us (22%)
  blocking collectives  95.1 us (17%)
  other arithmetic  61.1 us (11%)
  local copies, waits for them, and re-layouts  34.1 us (6%)
  starting transfers between devices  33.4 us (6%)
  between operations  15.5 us (3%)
    psum x1, waiting for transfers between devices, local(): summed = lax.psum((g_c, g_b, g_x, g_decay, g_bias, grad_gain_local), 'ctx')  99.3 us
    all_gather x2, waiting for transfers between devices, prefix(): pieces = jax.tree.map(lambda part: lax.all_gather(part, axis), value)  56.9 us
    dot_general x16, matrix products, update(): jnp.einsum('kglm,mkd->lkgd', weights, value_block.astype(jnp.float32), pr...  54.4 us
    select_n x30, other arithmetic, lap(): jnp.where(position < mine, new, old)  35.2 us
    psum x1, blocking collectives, local(): summed = lax.psum((g_c, g_b, g_x, g_decay, g_bias, grad_gain_local), 'ctx')  34.1 us
    unnamed x1, blocking collectives  33 us
    dot_general x16, matrix products, update(): jnp.einsum('lkgd,mkd->kglm', q_group, key_block, preferred_element_type=j...  24.9 us
    psum x1, blocking collectives, local(): lax.psum((jnp.sum(flat * flat, axis=1), jnp.sum(teacher_flat * teacher_fl...  15.6 us
  transfers between devices with their start and end apart: 10, of which 7 were waited for; matrix products, arithmetic and copies ran while one was open for 26% of the time, Pallas kernels for 0%

commit v1 on v0

v1 whole, which is shorter than its diff:
```python
import jax
import jax.numpy as jnp
from jax import lax
from jax.experimental import pallas as pl
from jax.experimental.pallas import tpu as pltpu
from jax.sharding import PartitionSpec as P

MESH = pl.DeviceIdType.MESH
F32 = jnp.float32
BF16 = jnp.bfloat16
HEADS = 8
DIM = 128
ROWS = 256
CTX = 16
TP = 8
CHIPS = CTX // 2
SUB = ROWS // CTX
PIECES = 4
PIECE = ROWS // PIECES
BLOCKS = CTX // PIECES
TOKENS = ROWS * CTX
FEATURES = HEADS * DIM * TP
EPS = 1e-05
SCALE = DIM**-0.5
LOG2E = 1.4426950408889634
PAIR = 2
NEG = -1e30


def nn(a, b):
    return lax.dot_general(a, b, (((1,), (0,)), ((), ())), preferred_element_type=F32)


def nt(a, b):
    return lax.dot_general(a, b, (((1,), (1,)), ((), ())), preferred_element_type=F32)


def split(value):
    high = value.astype(BF16)
    return high, (value - high.astype(F32)).astype(BF16)


def wide(value):
    return jnp.concatenate(split(value), axis=1)


def twice(value, axis):
    return jnp.concatenate([value, value], axis=axis)


def halves(value):
    return value[:, :DIM] + value[:, DIM:]


def by_mask(value, mask):
    first = value.astype(BF16)
    rest = value - first.astype(F32)
    second = rest.astype(BF16)
    third = (rest - second.astype(F32)).astype(BF16)
    return nn(first, mask) + nn(second, mask) + nn(third, mask)


def product(a, b):
    a_high, a_low = split(a)
    b_high, b_low = split(b)
    return halves(nn(a_high, jnp.concatenate([b_high, b_low], axis=1))) + nn(a_low, b_high)


def product_t(a, b):
    a_high, a_low = split(a)
    b_high, b_low = split(b)
    return nt(jnp.concatenate([a_high, a_low], axis=1), twice(b_high, 1)) + nt(a_high, b_low)


def iota(shape, axis):
    return lax.broadcasted_iota(jnp.int32, shape, axis)


def place(row):
    return (row & 15) * 16 + (row >> 4)


def columns_of(rows):
    return jnp.concatenate([rows, jnp.zeros((DIM - 8, ROWS), F32)], axis=0).T


def steps_of(logits, bias):
    raised = logits + bias
    faded = jnp.exp(-jnp.abs(raised))
    step = jnp.maximum(raised, 0.0) + jnp.log1p(faded)
    slope = jnp.where(raised >= 0.0, 1.0, faded) / (1.0 + faded)
    return step, slope


def kernel(
    q_in, k_in, v_in, z_in, decay_in, bias_in, c_w, b_w, x_w, gain_in,
    out, grad_c, grad_b, grad_x, grad_small,
    qr, kv, zall, kpos, vpos, qh, acc, top, tq, mom, wts, rows, rcol, rbcol, kown, vown,
    t_all, s_all, d_all, z_all, y_all, stats, stx, cols, decay_part, bias_part,
    gbuf, sibr, pairsum, rs, fin, small,
    local_sem, q_ss, q_rs, z_ss, z_rs, kv_ss, kv_rs, t_ss, t_rs, sib_ss, sib_rs, r_ss, r_rs,
    ag_ss, ag_rs, fw_ss, fw_rs, sm_ss, sm_rs,
):
    me = lax.axis_index("ctx")
    tp = lax.axis_index("tp")
    core = lax.rem(me, 2)
    chip = me // 2
    sibling = me + 1 - 2 * core

    def remote(src, dst, send, recv, where):
        return pltpu.make_async_remote_copy(
            src_ref=src, dst_ref=dst, send_sem=send, recv_sem=recv, device_id=where, device_id_type=MESH
        )

    def others(count, mine, body):
        def one(step, carry):
            body(lax.rem(mine + step, count))
            return carry

        lax.fori_loop(1, count, one, 0)

    def each(count, body):
        def one(step, carry):
            body(step)
            return carry

        lax.fori_loop(0, count, one, 0)

    def clear(source):
        kv[source] = jnp.zeros((ROWS, 2 * DIM), BF16)

    each(CTX, clear)
    own_rows = pl.ds(pl.multiple_of(SUB * me, SUB), SUB)
    own = [
        pltpu.make_async_copy(k_in, kv.at[me, :, pl.ds(0, DIM)], local_sem.at[0]),
        pltpu.make_async_copy(v_in, kv.at[me, :, pl.ds(DIM, DIM)], local_sem.at[1]),
        pltpu.make_async_copy(q_in.at[own_rows], qr.at[me], local_sem.at[2]),
    ]
    for copy in own:
        copy.start()
    zall[me] = z_in[...]
    barrier = pltpu.get_barrier_semaphore()
    others(CTX, me, lambda peer: pl.semaphore_signal(barrier, inc=1, device_id={"ctx": peer}, device_id_type=MESH))
    others(TP, tp, lambda peer: pl.semaphore_signal(barrier, inc=1, device_id={"tp": peer}, device_id_type=MESH))
    for copy in own:
        copy.wait()
    pl.semaphore_wait(barrier, CTX - 1 + TP - 1)

    def q_copy(peer, slot):
        taken = pl.ds(pl.multiple_of(SUB * peer, SUB), SUB)
        return remote(q_in.at[taken], qr.at[slot], q_ss.at[peer], q_rs.at[slot], {"ctx": peer})

    def z_copy(peer, slot):
        return remote(zall.at[slot], zall.at[slot], z_ss.at[peer], z_rs.at[slot], {"ctx": peer})

    def kv_copy(peer, slot, piece):
        part = pl.ds(pl.multiple_of(PIECE * piece, PIECE), PIECE)
        return remote(
            kv.at[slot, part], kv.at[slot, part], kv_ss.at[peer, piece], kv_rs.at[slot, piece], {"ctx": peer}
        )

    others(CTX, me, lambda peer: z_copy(peer, me).start())
    others(CTX, me, lambda peer: q_copy(peer, me).start())

    def send_piece(piece):
        def send(peer):
            @pl.when(peer >= BLOCKS * piece)
            def _():
                kv_copy(peer, me, piece).start()

        others(CTX, me, send)

    each(PIECES, send_piece)

    others(CTX, me, lambda peer: z_copy(peer, peer).wait_recv())
    logits = zall[...]
    speed = -jnp.exp(decay_in[...])
    step, slope = steps_of(logits, bias_in[...][None])
    rate = speed[None] * step
    rate_b = speed[None] * slope
    lower = iota((ROWS, ROWS), 0)
    upper = iota((ROWS, ROWS), 1)
    after = jnp.where((lower > upper) & (lower < SUB * me), 1.0, 0.0).astype(BF16)
    span = by_mask(jnp.sum(rate, axis=0), after)
    span_b = by_mask(jnp.sum(rate_b, axis=0), after)
    earlier = iota((HEADS, ROWS), 1) < SUB * me
    for source in reversed(range(CTX)):
        weight = jnp.where(earlier, jnp.exp(span) * step[source], 0.0)
        wts[0, source] = weight
        wts[1, source] = weight * span
        wts[2, source] = weight * (span_b + slope[source] / step[source])
        span = span + rate[source]
        span_b = span_b + rate_b[source]

    pick = jnp.where(lower == SUB * me + (upper & 15), 1.0, 0.0).astype(BF16)
    picked = nn(logits.reshape(CTX * HEADS, ROWS).astype(BF16), pick).reshape(CTX, HEADS, ROWS)
    matched = iota((CTX, HEADS, ROWS), 0) == (iota((CTX, HEADS, ROWS), 2) >> 4)
    own_logits = jnp.sum(jnp.where(matched, picked, 0.0), axis=0)
    own_step, own_slope = steps_of(own_logits, bias_in[...])
    until = jnp.where(place(lower) <= place(upper), 1.0, 0.0).astype(BF16)
    running = by_mask(speed * own_step, until)
    running_b = by_mask(speed * own_slope, until)
    rows[0] = running
    rows[1] = own_step
    rows[2] = running_b
    rows[3] = own_slope / own_step
    running_c = columns_of(running)
    running_bc = columns_of(running_b)
    for head in range(HEADS):
        rcol[head] = jnp.broadcast_to(running_c[:, head : head + 1], (ROWS, DIM))
        rbcol[head] = jnp.broadcast_to(running_bc[:, head : head + 1], (ROWS, DIM))

    others(CTX, me, lambda peer: q_copy(peer, peer).wait_recv())
    for head in range(HEADS):
        qh[head] = qr[:, :, head * DIM : (head + 1) * DIM].reshape(ROWS, DIM)
        acc[head] = jnp.zeros((ROWS, 2 * DIM), F32)
        top[head] = jnp.full((ROWS, DIM), NEG, F32)

    def attend(chunk, group, masked):
        heads = pl.ds(PAIR * group, PAIR)
        query = qh[heads].reshape(PAIR * ROWS, DIM)
        key = kpos[pl.ds(2 * chunk, 2)].reshape(2 * ROWS, DIM)
        value = vpos[pl.ds(2 * chunk, 2)].reshape(2 * ROWS, 2 * DIM)
        scores = nt(query, key) * (SCALE * LOG2E)
        if masked:
            at_q = place(iota(scores.shape, 0) & (ROWS - 1)) + ROWS * me
            lane = iota(scores.shape, 1)
            at_k = place(lane & (ROWS - 1)) + (lane >> 8) * ROWS + 2 * ROWS * chunk
            scores = jnp.where(at_k <= at_q, scores, NEG)
        old = top[heads].reshape(PAIR * ROWS, DIM)
        new = jnp.maximum(old, jnp.max(scores, axis=1, keepdims=True))
        weights = jnp.exp2(scores - new[:, :1])
        shrink = jnp.exp2(old - new)
        mixed = nn(weights.astype(BF16), value)
        total = acc[heads].reshape(PAIR * ROWS, 2 * DIM)
        acc[heads] = (total * twice(shrink, 1) + mixed).reshape(PAIR, ROWS, 2 * DIM)
        top[heads] = new.reshape(PAIR, ROWS, DIM)

    def fold_piece(piece):
        def arrived(peer):
            kv_copy(peer, peer, piece).wait_recv()

        others(CTX, me, arrived)

        def sort(index):
            block = BLOCKS * piece + index
            part = pl.ds(pl.multiple_of(SUB * block, SUB), SUB)
            both = kv[:, part, :].reshape(ROWS, 2 * DIM)
            kpos[block] = both[:, :DIM]
            vpos[block, :, :DIM] = both[:, DIM:]
            vpos[block, :, DIM:] = jnp.ones((ROWS, DIM), BF16)

        each(BLOCKS, sort)

        def over(chunk, carry):
            each(HEADS // PAIR, lambda group: attend(chunk, group, False))
            return carry

        first = piece * (BLOCKS // 2)
        lax.fori_loop(first, jnp.minimum(first + BLOCKS // 2, chip), over, 0)

    each(me // BLOCKS + 1, fold_piece)
    each(HEADS // PAIR, lambda group: attend(chip, group, True))

    def close(head):
        total = acc[head]
        tq[head] = (total[:, :DIM] / total[:, DIM:]).astype(BF16)

    each(HEADS, close)

    mom[...] = jnp.zeros_like(mom)

    def moments(source):
        both = kv[source]
        key_t = both[:, :DIM].astype(F32).T
        value = both[:, DIM:]
        for head in range(HEADS):
            high, low = split(key_t * wts[0, source, head : head + 1, :])
            by_decay = (key_t * wts[1, source, head : head + 1, :]).astype(BF16)
            by_bias = (key_t * wts[2, source, head : head + 1, :]).astype(BF16)
            stacked = jnp.concatenate([high, low, by_decay, by_bias], axis=0)
            mom[head] = mom[head] + nn(stacked, value)

    each(CTX, moments)

    own_kv = kv[:, own_rows, :].reshape(ROWS, 2 * DIM)
    kown[...] = twice(own_kv[:, :DIM], 1)
    vown[...] = twice(own_kv[:, DIM:], 1)
    stats[...] = jnp.zeros_like(stats)

    def decays(head):
        causal = place(iota((ROWS, ROWS), 1)) <= place(iota((ROWS, ROWS), 0))
        gap = twice(rcol[head], 1) - rows[0, pl.ds(head, 1), :]
        return jnp.where(causal, jnp.exp(gap), 0.0) * rows[1, pl.ds(head, 1), :]

    def forward(head):
        mapped = wide(nt(c_w[head], b_w[head]) * SCALE)
        read = halves(nn(qh[head], mapped))
        t_all[head] = read
        score = nt(wide(read), kown[...])
        s_all[head] = score
        decay = decays(head)
        d_all[head] = decay
        high, low = split(score * decay)
        value = vown[:, :DIM]
        state = mom[head, 0:DIM] + mom[head, DIM : 2 * DIM]
        mixed = nn(high, value) + nn(low, value) + jnp.exp(rcol[head]) * product(read, state)
        z_all[head] = mixed
        flat = nn(wide(mixed), twice(x_w[head], 0))
        y_all[head] = flat
        taught = tq[head].astype(F32)
        scaled = flat * gain_in[pl.ds(head, 1), :]
        stats[0] += flat * flat
        stats[1] += taught * taught
        stats[2] += scaled * scaled
        stats[3] += scaled * taught

    each(HEADS, forward)

    lane = iota((ROWS, DIM), 1)
    packed = jnp.zeros((ROWS, DIM), F32)
    for index in range(4):
        packed = jnp.where(lane == index, jnp.sum(stats[index], axis=1, keepdims=True), packed)
    stx[tp] = packed.T[:8]

    def t_copy(peer, slot):
        return remote(stx.at[slot], stx.at[slot], t_ss.at[peer], t_rs.at[slot], {"tp": peer})

    others(TP, tp, lambda peer: t_copy(peer, tp).start())
    others(TP, tp, lambda peer: t_copy(peer, peer).wait_recv())
    sums = jnp.sum(stx[...], axis=0)
    inverse = lax.rsqrt(sums[0:1] / FEATURES + EPS)
    inverse_t = lax.rsqrt(sums[1:2] / FEATURES + EPS)
    cross = (2.0 / TOKENS) * (inverse * sums[2:3] - inverse_t * sums[3:4])
    pull = inverse * inverse * inverse * cross / FEATURES
    line = iota((8, ROWS), 0)
    spread = columns_of(jnp.where(line == 0, inverse, jnp.where(line == 1, inverse_t, pull)))
    for index in range(3):
        cols[index] = jnp.broadcast_to(spread[:, index : index + 1], (ROWS, DIM))

    order = jnp.where(iota((ROWS, ROWS), 0) == place(iota((ROWS, ROWS), 1)), 1.0, 0.0).astype(BF16)

    def sib_copy(head):
        return remote(gbuf.at[1 - core, head], sibr.at[head], sib_ss.at[head], sib_rs.at[head], {"ctx": sibling})

    def r_copy(head, slot):
        return remote(pairsum.at[head], rs.at[slot], r_ss.at[head], r_rs.at[slot], {"ctx": 2 * head + core})

    def pass_on(head):
        sib_copy(head).wait_recv()
        pairsum[head] = gbuf[core, head] + sibr[head]

        @pl.when(head != chip)
        def _():
            r_copy(head, chip).start()

        @pl.when(head == chip)
        def _():
            rs[chip] = pairsum[head]

    def backward(head):
        flat = y_all[head]
        gain = gain_in[pl.ds(head, 1), :]
        inv = cols[0]
        unit = flat * inv
        normed = unit * gain
        out[:, pl.ds(pl.multiple_of(head * DIM, DIM), DIM)] = nn(order, normed.astype(BF16)).astype(BF16)
        d_normed = (2.0 / TOKENS) * (normed - tq[head].astype(F32) * cols[1])
        small[me, pl.ds(head, 1), :] = jnp.sum(d_normed * unit, axis=0, keepdims=True)
        d_flat = d_normed * gain * inv - flat * cols[2]
        moved = d_flat * flat
        run = rcol[head]
        by_decay = jnp.sum(moved * run, axis=0, keepdims=True)
        by_bias = jnp.sum(moved * rbcol[head], axis=0, keepdims=True)
        mixed = z_all[head]
        gbuf[1, head] = product(mixed.T, d_flat)
        d_mixed = nt(wide(d_flat), twice(x_w[head], 1))
        d_score = nt(wide(d_mixed), vown[...]) * d_all[head]
        felt = jnp.sum(d_score * s_all[head], axis=0, keepdims=True)
        from_decay = felt * rows[0, pl.ds(head, 1), :]
        from_bias = felt * (rows[3, pl.ds(head, 1), :] - rows[2, pl.ds(head, 1), :])
        by_decay = by_decay - halves(from_decay)
        by_bias = by_bias + halves(from_bias)
        high, low = split(d_score)
        key = kown[:, :DIM]
        d_late = jnp.exp(run) * d_mixed
        state = mom[head, 0:DIM] + mom[head, DIM : 2 * DIM]
        d_read = nn(high, key) + nn(low, key) + product_t(d_late, state)
        d_state = product(t_all[head].T, d_late)
        by_decay = by_decay + jnp.sum(d_state * mom[head, 2 * DIM : 3 * DIM], axis=0, keepdims=True)
        by_bias = by_bias + jnp.sum(d_state * mom[head, 3 * DIM : 4 * DIM], axis=0, keepdims=True)
        decay_part[pl.ds(head, 1), :] = by_decay
        bias_part[pl.ds(head, 1), :] = by_bias
        query_t = qh[head].astype(F32).T.astype(BF16)
        gbuf[0, head] = halves(nn(query_t, wide(d_read)))
        sib_copy(head).start()

        @pl.when(head > 0)
        def _():
            pass_on(head - 1)

    each(HEADS, backward)
    pass_on(HEADS - 1)
    line = iota((HEADS, DIM), 1)
    decay_sum = jnp.sum(decay_part[...], axis=1, keepdims=True)
    bias_sum = jnp.sum(bias_part[...], axis=1, keepdims=True)
    small[me, HEADS:, :] = jnp.where(line == 0, decay_sum, jnp.where(line == 1, bias_sum, 0.0))

    def sm_copy(peer, slot):
        return remote(small.at[slot], small.at[slot], sm_ss.at[peer], sm_rs.at[slot], {"ctx": peer})

    others(CTX, me, lambda peer: sm_copy(peer, me).start())

    others(CHIPS, chip, lambda peer: r_copy(peer, peer).wait_recv())
    fin[core, chip] = jnp.sum(rs[...], axis=0)

    def ag_copy(peer, slot):
        held = fin.at[core, slot]
        return remote(held, held, ag_ss.at[peer], ag_rs.at[slot], {"ctx": 2 * peer + core})

    def fw_copy(slot, side):
        held = fin.at[side, slot]
        return remote(held, held, fw_ss.at[slot], fw_rs.at[slot], {"ctx": sibling})

    others(CHIPS, chip, lambda peer: ag_copy(peer, chip).start())
    fw_copy(chip, core).start()

    def hand_over(peer):
        ag_copy(peer, peer).wait_recv()
        fw_copy(peer, core).start()

    others(CHIPS, chip, hand_over)

    def finish(head):
        fw_copy(head, 1 - core).wait_recv()
        grad_x[head] = fin[1, head]
        joint = fin[0, head]
        grad_c[head] = nn(wide(joint), twice(b_w[head], 0)) * SCALE
        grad_b[head] = nn(wide(joint.T), twice(c_w[head], 0)) * SCALE

    each(HEADS, finish)
    others(CTX, me, lambda peer: sm_copy(peer, peer).wait_recv())
    grad_small[...] = jnp.sum(small[...], axis=0)

    def left(peer):
        z_copy(peer, me).wait_send()
        q_copy(peer, me).wait_send()
        sm_copy(peer, me).wait_send()

    others(CTX, me, left)

    def left_piece(piece):
        def one(peer):
            @pl.when(peer >= BLOCKS * piece)
            def _():
                kv_copy(peer, me, piece).wait_send()

        others(CTX, me, one)

    each(PIECES, left_piece)
    others(TP, tp, lambda peer: t_copy(peer, tp).wait_send())
    others(CHIPS, chip, lambda peer: r_copy(peer, chip).wait_send())
    others(CHIPS, chip, lambda peer: ag_copy(peer, chip).wait_send())

    def left_pair(head):
        sib_copy(head).wait_send()
        fw_copy(head, core).wait_send()

    each(HEADS, left_pair)


def local(queries, keys, values, dt_logits, decay_log, dt_bias, c_weight, b_weight, x_weight, norm_gain):
    whole = pl.BlockSpec(memory_space=pltpu.VMEM)
    there = pl.BlockSpec(memory_space=pl.ANY)
    dma = pltpu.SemaphoreType.DMA

    def f32(*shape):
        return pltpu.VMEM(shape, F32)

    def bf16(*shape):
        return pltpu.VMEM(shape, BF16)

    square = (HEADS, DIM, DIM)
    by_row = (HEADS, ROWS, DIM)
    out, grad_c, grad_b, grad_x, small = pl.pallas_call(
        kernel,
        out_shape=(
            jax.ShapeDtypeStruct((ROWS, HEADS * DIM), BF16),
            jax.ShapeDtypeStruct(square, F32),
            jax.ShapeDtypeStruct(square, F32),
            jax.ShapeDtypeStruct(square, F32),
            jax.ShapeDtypeStruct((2 * HEADS, DIM), F32),
        ),
        in_specs=[there] * 3 + [whole] * 7,
        out_specs=[whole] * 5,
        scratch_shapes=[
            bf16(CTX, SUB, HEADS * DIM),
            bf16(CTX, ROWS, 2 * DIM),
            f32(CTX, HEADS, ROWS),
            bf16(CTX, ROWS, DIM),
            bf16(CTX, ROWS, 2 * DIM),
            bf16(*by_row),
            f32(HEADS, ROWS, 2 * DIM),
            f32(*by_row),
            bf16(*by_row),
            f32(HEADS, 4 * DIM, DIM),
            f32(3, CTX, HEADS, ROWS),
            f32(4, HEADS, ROWS),
            f32(*by_row),
            f32(*by_row),
            bf16(ROWS, 2 * DIM),
            bf16(ROWS, 2 * DIM),
            f32(*by_row),
            f32(HEADS, ROWS, ROWS),
            f32(HEADS, ROWS, ROWS),
            f32(*by_row),
            f32(*by_row),
            f32(4, ROWS, DIM),
            f32(TP, 8, ROWS),
            f32(3, ROWS, DIM),
            f32(HEADS, DIM),
            f32(HEADS, DIM),
            f32(2, *square),
            f32(*square),
            f32(*square),
            f32(CHIPS, DIM, DIM),
            f32(2, *square),
            f32(CTX, 2 * HEADS, DIM),
            dma((3,)),
            dma((CTX,)), dma((CTX,)), dma((CTX,)), dma((CTX,)),
            dma((CTX, PIECES)), dma((CTX, PIECES)),
            dma((TP,)), dma((TP,)),
            dma((HEADS,)), dma((HEADS,)), dma((CHIPS,)), dma((CHIPS,)),
            dma((CHIPS,)), dma((CHIPS,)), dma((HEADS,)), dma((HEADS,)),
            dma((CTX,)), dma((CTX,)),
        ],
        compiler_params=pltpu.CompilerParams(
            collective_id=0, has_side_effects=True, vmem_limit_bytes=56 * 2**20
        ),
    )(
        queries, keys, values, dt_logits.astype(F32).T, decay_log.reshape(HEADS, 1), dt_bias.reshape(HEADS, 1),
        c_weight, b_weight, x_weight, norm_gain.reshape(HEADS, DIM),
    )
    return out, grad_c, grad_b, grad_x, small[HEADS:, 0], small[HEADS:, 1], small[:HEADS].reshape(-1)


def solution(mesh):
    return jax.shard_map(
        local,
        mesh=mesh,
        in_specs=(
            P("ctx", "tp"),
            P("ctx", "tp"),
            P("ctx", "tp"),
            P("ctx", "tp"),
            P("tp"),
            P("tp"),
            P("tp", None, None),
            P("tp", None, None),
            P("tp", None, None),
            P("tp"),
        ),
        out_specs=(
            P("ctx", "tp"),
            P("tp", None, None),
            P("tp", None, None),
            P("tp", None, None),
            P("tp"),
            P("tp"),
            P("tp"),
        ),
        check_vma=False,
    )
```

time: 550 us -> 130 us (0.24); the launches traced: 540 us -> 130 us
  waiting for transfers between devices: 179 us -> 0 us
  matrix products: 120 us -> 0 us
  Pallas kernels: 0 us -> 118 us
  blocking collectives: 95.1 us -> 0 us
  other arithmetic: 61.1 us -> 1.29 us
  starting transfers between devices: 33.4 us -> 0 us
  local copies, waits for them, and re-layouts: 34.1 us -> 9.93 us
  between operations: 15.5 us -> 0.66 us
    dot_general x52 -> x0, matrix products: 120 us -> none  [the longest x16 54.4 us: update(): jnp.einsum('kglm,mkd->lkgd', weights, value_block.astype(jnp.float32), pr...]
    pallas_call x0 -> x1, Pallas kernels: none -> 118 us  [local(): pl.pallas_call(kernel, out_shape=(jax.ShapeDtypeStruct((ROWS, HEADS * DIM...]
    psum x1 -> x0, waiting for transfers between devices: 99.3 us -> none  [local(): summed = lax.psum((g_c, g_b, g_x, g_decay, g_bias, grad_gain_local), 'ctx')]
    psum x3 -> x0, blocking collectives: 62.1 us -> none  [the longest x1 34.1 us: local(): summed = lax.psum((g_c, g_b, g_x, g_decay, g_bias, grad_gain_local), 'ctx')]
    all_gather x4 -> x0, waiting for transfers between devices: 59.8 us -> none  [the longest x2 56.9 us: prefix(): pieces = jax.tree.map(lambda part: lax.all_gather(part, axis), value)]
    select_n x30 -> x0, other arithmetic: 35.2 us -> none  [lap(): jnp.where(position < mine, new, old)]
    unnamed x1 -> x0, blocking collectives: 33 us -> none
    all_to_all x5 -> x0, starting transfers between devices: 32.6 us -> none  [the longest x1 9.46 us: local(): lax.all_to_all(regroup(dt_logits, ctx_ways), 'ctx', split_axis=0, concat_...]
  transfers between devices with their start and end apart: 10 -> 0, of which waited for: 7 -> 0; matrix products, arithmetic and copies ran while one was open for 26% -> 0% of each run, Pallas kernels for 0% -> 0%
where the time goes in v1:
time: 130 us
  Pallas kernels  118 us (91%)
  local copies, waits for them, and re-layouts  9.93 us (8%)
    pallas_call x1, Pallas kernels, local(): pl.pallas_call(kernel, out_shape=(jax.ShapeDtypeStruct((ROWS, HEADS * DIM...  118 us
    unnamed x16, local copies, waits for them, and re-layouts  6.5 us

profile of v1, /device:TPU:1, one launch (start us, length us, event | category | flops | bytes accessed | tf_op | source)
XLA Modules:
  0.0 129.9 jit_solution(3796152150447738343)
XLA Ops:
  0.6 1.3 convert_bitcast_fusion.z_in
  1.9 0.0 copy-start.4
  1.9 0.7 copy-done.4
  2.6 0.7 copy.19.decay_in
  3.2 0.0 copy-start.5
  3.2 0.7 copy-done.5
  3.9 0.7 copy.20.bias_in
  4.6 118.1 %shard_map.153 = (bf16[256,1024]{1,0:T(8,128)(2,1)}, f32[8,128,128]{2,1,0:T(8,128)}, f32[8,128,128]{2,1,0:T(8,128)}, f32[8,128,128]{2,1,0:T(8,128)}, f32[16,128]{1,0:T(8,128)}) custom-call(bf16[256,1024]{1,0:T(8,128)(2,1)} %q_in.1, bf16[256,128]{1,0:T(8,128)(2,1)} %k_in.1, bf16[256,128]{1,0:T(8,128)(2,1)} %v_in.1, f32[8,256]{1,0:T(8,128)} %convert_bitcast_fusion.z_in, ...), custom_call_target="tpu_custom_call" | custom-call | tf_op jit(solution)/shard_map/pallas_call | solution.py:485
  122.6 0.0 copy-start.3
  122.6 1.5 %slice_reduce_fusion = (f32[8]{0:T(128)}, f32[8]{0:T(128)}) fusion(f32[16,128]{1,0:T(8,128)} %get-tuple-element.16), kind=kLoop, calls=%fused_computation.2 | loop fusion | bytes 128 | tf_op jit(solution)/shard_map/slice | solution.py:544
  124.1 0.0 copy-done.3
  124.1 0.6 slice_bitcast_fusion
  124.7 0.0 copy-start.2
  124.7 1.9 %copy.25 = bf16[256,1024]{1,0:T(8,128)(2,1)} copy(bf16[256,1024]{1,0:T(8,128)(2,1)} %get-tuple-element.26) | data formatting | bytes 1048576
  126.7 0.0 copy-done.2
  126.7 0.0 copy-start.1
  126.7 0.8 copy.26
  127.5 0.4 copy-done.1
  127.9 0.0 copy-start
  127.9 0.8 copy.27
  128.7 0.4 copy-done
  129.1 0.8 copy.28
Async XLA Ops:
  1.9 0.7 copy-start.4
  3.2 0.7 copy-start.5
  122.6 1.5 %copy-start.3 = (f32[16,128]{1,0:T(8,128)S(1)}, f32[16,128]{1,0:T(8,128)}, u32[]{:S(2)}) copy-start(f32[16,128]{1,0:T(8,128)} %get-tuple-element.16) | copy-start | bytes 24580
  124.7 1.9 %copy-start.2 = (f32[8,128,128]{2,1,0:T(8,128)S(1)}, f32[8,128,128]{2,1,0:T(8,128)}, u32[]{:S(2)}) copy-start(f32[8,128,128]{2,1,0:T(8,128)} %get-tuple-element.27) | copy-start | bytes 1572868
  126.7 1.2 copy-start.1
  127.9 1.2 copy-start

commit v2 on v1

v2 whole, which is shorter than its diff:
```python
import jax
import jax.numpy as jnp
from jax import lax
from jax.experimental import pallas as pl
from jax.experimental.pallas import tpu as pltpu
from jax.sharding import PartitionSpec as P

MESH = pl.DeviceIdType.MESH
F32 = jnp.float32
BF16 = jnp.bfloat16
HEADS = 8
DIM = 128
ROWS = 256
CTX = 16
TP = 8
CHIPS = CTX // 2
SUB = ROWS // CTX
PIECES = 2
PIECE = ROWS // PIECES
WIDTH = 4
STEPS = CTX // PIECES // WIDTH
QUAD = 4
HEAD_ROWS = 16
TAIL = 8
GROUP = 2
TOKENS = ROWS * CTX
FEATURES = HEADS * DIM * TP
EPS = 1e-05
SCALE = DIM**-0.5
LOG2E = 1.4426950408889634
NEG = -1e30


def nn(a, b):
    return lax.dot_general(a, b, (((1,), (0,)), ((), ())), preferred_element_type=F32)


def nt(a, b):
    return lax.dot_general(a, b, (((1,), (1,)), ((), ())), preferred_element_type=F32)


def split(value):
    high = value.astype(BF16)
    return high, (value - high.astype(F32)).astype(BF16)


def wide(value):
    return jnp.concatenate(split(value), axis=1)


def twice(value, axis):
    return jnp.concatenate([value, value], axis=axis)


def halves(value):
    return value[:, :DIM] + value[:, DIM:]


def by_mask(value, mask):
    first = value.astype(BF16)
    rest = value - first.astype(F32)
    second = rest.astype(BF16)
    third = (rest - second.astype(F32)).astype(BF16)
    return nn(first, mask) + nn(second, mask) + nn(third, mask)


def product(a, b):
    a_high, a_low = split(a)
    b_high, b_low = split(b)
    return halves(nn(a_high, jnp.concatenate([b_high, b_low], axis=1))) + nn(a_low, b_high)


def product_t(a, b):
    a_high, a_low = split(a)
    b_high, b_low = split(b)
    return nt(jnp.concatenate([a_high, a_low], axis=1), twice(b_high, 1)) + nt(a_high, b_low)


def iota(shape, axis):
    return lax.broadcasted_iota(jnp.int32, shape, axis)


def place(row):
    return (row & 15) * 16 + (row >> 4)


def columns_of(rows):
    return jnp.concatenate([rows, jnp.zeros((DIM - 8, ROWS), F32)], axis=0).T


def steps_of(logits, bias):
    raised = logits + bias
    faded = jnp.exp(-jnp.abs(raised))
    step = jnp.maximum(raised, 0.0) + jnp.log1p(faded)
    slope = jnp.where(raised >= 0.0, 1.0, faded) / (1.0 + faded)
    return step, slope


def kernel(
    q_in, k_in, v_in, z_in, decay_in, bias_in, c_in, b_in, x_in, gain_in,
    out_to, fin_to,
    qr, kv, kpos, vpos, qh, hide, acc, top, tq, mom, tangent, wts, rows, rcol, rbcol, kown, vown, gains,
    c_w, b_w, x_w, t_all, s_all, d_all, z_all, y_all, stats, stx, cols, out,
    gbuf, sibr, pairsum, rs, fin,
    local_sem, w_sem, out_sem, q_ss, q_rs, kv_ss, kv_rs, kf_ss, kf_rs, t_ss, t_rs, sib_ss, sib_rs, r_ss, r_rs,
    ag_ss, ag_rs, fw_ss, fw_rs,
):
    me = lax.axis_index("ctx")
    tp = lax.axis_index("tp")
    core = lax.rem(me, 2)
    chip = me // 2
    sibling = me + 1 - 2 * core

    def remote(src, dst, send, recv, where):
        return pltpu.make_async_remote_copy(
            src_ref=src, dst_ref=dst, send_sem=send, recv_sem=recv, device_id=where, device_id_type=MESH
        )

    def others(count, mine, body):
        for step in range(1, count):
            body((mine + step) & (count - 1))

    def each(count, body):
        def one(step, carry):
            body(step)
            return carry

        lax.fori_loop(0, count, one, 0)

    own_rows = pl.ds(pl.multiple_of(SUB * me, SUB), SUB)
    body_rows = pl.ds(HEAD_ROWS, ROWS)
    own = [
        pltpu.make_async_copy(k_in, kv.at[me, body_rows, pl.ds(0, DIM)], local_sem.at[0]),
        pltpu.make_async_copy(v_in, kv.at[me, body_rows, pl.ds(DIM, DIM)], local_sem.at[1]),
        pltpu.make_async_copy(q_in.at[own_rows], qr.at[me], local_sem.at[2]),
    ]
    for copy in own:
        copy.start()
    weights = [
        pltpu.make_async_copy(c_in, c_w, w_sem.at[0]),
        pltpu.make_async_copy(b_in, b_w, w_sem.at[1]),
        pltpu.make_async_copy(x_in, x_w, w_sem.at[2]),
    ]
    for copy in weights:
        copy.start()
    barrier = pltpu.get_barrier_semaphore()
    others(CTX, me, lambda peer: pl.semaphore_signal(barrier, inc=1, device_id={"ctx": peer}, device_id_type=MESH))
    others(TP, tp, lambda peer: pl.semaphore_signal(barrier, inc=1, device_id={"tp": peer}, device_id_type=MESH))
    turn = jnp.where(iota((HEAD_ROWS, HEADS), 0) == iota((HEAD_ROWS, HEADS), 1), 1.0, 0.0).astype(BF16)
    kv[me, :HEAD_ROWS, :] = nt(turn, z_in[...]).astype(BF16)
    for copy in own:
        copy.wait()
    pl.semaphore_wait(barrier, CTX - 1 + TP - 1)

    def part_of(piece):
        if piece == 0:
            return pl.ds(0, HEAD_ROWS + PIECE)
        return pl.ds(HEAD_ROWS + PIECE * piece, PIECE)

    def kv_copy(peer, slot, piece):
        held = kv.at[2 * slot + core, part_of(piece)]
        return remote(held, held, kv_ss.at[peer, piece], kv_rs.at[slot, piece], {"ctx": 2 * peer + core})

    def kf_copy(slot, side, piece):
        held = kv.at[2 * slot + side, part_of(piece)]
        return remote(held, held, kf_ss.at[slot, piece], kf_rs.at[slot, piece], {"ctx": sibling})

    def needs(peer, piece):
        return peer >= piece * (CHIPS // PIECES)

    def q_copy(peer, slot):
        taken = pl.ds(pl.multiple_of(SUB * peer, SUB), SUB)
        return remote(q_in.at[taken], qr.at[slot], q_ss.at[peer], q_rs.at[slot], {"ctx": peer})

    def send_piece(piece):
        def send(peer):
            @pl.when(needs(peer, piece))
            def _():
                kv_copy(peer, chip, piece).start()

        others(CHIPS, chip, send)

        @pl.when(needs(chip, piece))
        def _():
            kf_copy(chip, core, piece).start()

    def relay(piece):
        def one(peer):
            kv_copy(peer, peer, piece).wait_recv()
            kf_copy(peer, core, piece).start()

        others(CHIPS, chip, one)

    def arrived(piece):
        kf_copy(chip, 1 - core, piece).wait_recv()
        others(CHIPS, chip, lambda peer: kf_copy(peer, 1 - core, piece).wait_recv())

    send_piece(0)
    others(CTX, me, lambda peer: q_copy(peer, me).start())
    for piece in range(1, PIECES):
        send_piece(piece)

    for head in range(HEADS):
        gains[head : head + 1, :] = gain_in[head * DIM : (head + 1) * DIM].reshape(1, DIM)
        acc[head] = jnp.zeros((ROWS, 2 * DIM), F32)
        top[head] = jnp.full((ROWS, DIM), NEG, F32)
    mom[...] = jnp.zeros_like(mom)
    tangent[...] = jnp.zeros_like(tangent)
    stats[...] = jnp.zeros_like(stats)
    last = me // WIDTH
    shown = (ROWS, WIDTH * ROWS)
    key_place = place(iota(shown, 1) & (ROWS - 1)) + (iota(shown, 1) >> 8) * ROWS + WIDTH * ROWS * last
    hide[...] = jnp.where(key_place <= place(iota(shown, 0)) + ROWS * me, 0.0, NEG)
    head_line = iota((HEADS, ROWS), 0)
    decay_rate = jnp.zeros((HEADS, ROWS), F32)
    bias = jnp.zeros((HEADS, ROWS), F32)
    for head in range(HEADS):
        decay_rate = jnp.where(head_line == head, decay_in[head], decay_rate)
        bias = jnp.where(head_line == head, bias_in[head], bias)
    speed = -jnp.exp(decay_rate)
    relay(0)
    arrived(0)

    logits = kv[:, :HEAD_ROWS, :].astype(F32)[:, :HEADS, :]
    step, slope = steps_of(logits, bias[None])
    rate = speed[None] * step
    rate_b = speed[None] * slope
    lower = iota((ROWS, ROWS), 0)
    upper = iota((ROWS, ROWS), 1)
    after = jnp.where((lower > upper) & (lower < SUB * me), 1.0, 0.0).astype(BF16)
    span = by_mask(jnp.sum(rate, axis=0), after)
    span_b = by_mask(jnp.sum(rate_b, axis=0), after)
    earlier = iota((HEADS, ROWS), 1) < SUB * me
    for source in reversed(range(CTX)):
        weight = jnp.where(earlier, jnp.exp(span) * step[source], 0.0)
        kinds = (weight, weight * span, weight * (span_b + slope[source] / step[source]))
        for index, kind in enumerate(kinds):
            for piece in range(PIECES):
                wts[index, piece, :, source * PIECE : (source + 1) * PIECE] = kind[:, piece * PIECE : (piece + 1) * PIECE]
        span = span + rate[source]
        span_b = span_b + rate_b[source]

    pick = jnp.where(lower == SUB * me + (upper & 15), 1.0, 0.0).astype(BF16)
    picked = nn(logits.reshape(CTX * HEADS, ROWS).astype(BF16), pick).reshape(CTX, HEADS, ROWS)
    matched = iota((CTX, HEADS, ROWS), 0) == (iota((CTX, HEADS, ROWS), 2) >> 4)
    own_logits = jnp.sum(jnp.where(matched, picked, 0.0), axis=0)
    own_step, own_slope = steps_of(own_logits, bias)
    until = jnp.where(place(lower) <= place(upper), 1.0, 0.0).astype(BF16)
    running = by_mask(speed * own_step, until)
    running_b = by_mask(speed * own_slope, until)
    rows[0] = running
    rows[1] = own_step
    rows[2] = running_b
    rows[3] = own_slope / own_step
    running_c = columns_of(running)
    running_bc = columns_of(running_b)
    for head in range(HEADS):
        rcol[head] = jnp.broadcast_to(running_c[:, head : head + 1], (ROWS, DIM))
        rbcol[head] = jnp.broadcast_to(running_bc[:, head : head + 1], (ROWS, DIM))

    def gathered(piece, quad):
        part = kv[pl.ds(QUAD * quad, QUAD), pl.ds(HEAD_ROWS + PIECE * piece, PIECE), :]
        both = part.reshape(QUAD * PIECE, 2 * DIM)
        lanes = pl.ds(pl.multiple_of(quad * QUAD * PIECE, QUAD * PIECE), QUAD * PIECE)
        return both[:, :DIM].astype(F32).T, both[:, DIM:], lanes

    def moments(piece):
        def one(quad):
            key_t, value, lanes = gathered(piece, quad)
            double = twice(value, 0)
            for head in range(HEADS):
                mom[head] += nn(wide(key_t * wts[0, piece, head : head + 1, lanes]), double)

        each(CTX // QUAD, one)

    def tangents(piece):
        def one(quad):
            key_t, value, lanes = gathered(piece, quad)
            for head in range(HEADS):
                by_decay = (key_t * wts[1, piece, head : head + 1, lanes]).astype(BF16)
                by_bias = (key_t * wts[2, piece, head : head + 1, lanes]).astype(BF16)
                tangent[head] += nn(jnp.concatenate([by_decay, by_bias], axis=0), value)

        each(CTX // QUAD, one)

    def sort(piece):
        def one(index):
            block = piece * (CTX // PIECES) + index
            part = pl.ds(pl.multiple_of(HEAD_ROWS + SUB * block, SUB), SUB)
            both = kv[:, part, :].reshape(ROWS, 2 * DIM)
            kpos[block] = both[:, :DIM]
            vpos[block, :, :DIM] = both[:, DIM:]
            vpos[block, :, DIM:] = jnp.ones((ROWS, DIM), BF16)

        each(CTX // PIECES, one)

    def attend(chunk, masked):
        blocks = pl.ds(WIDTH * chunk, WIDTH)
        key = kpos[blocks].reshape(WIDTH * ROWS, DIM)
        value = vpos[blocks].reshape(WIDTH * ROWS, 2 * DIM)

        def mix(head, weights, shrink):
            acc[head] = acc[head] * twice(shrink, 1) + nn(weights, value)

        scores = nt(qh[0], key)
        waiting = None
        for head in range(HEADS):
            following = nt(qh[head + 1], key) if head + 1 < HEADS else None
            if masked:
                scores = scores + hide[...]
            old = top[head]
            new = jnp.maximum(old, jnp.max(scores, axis=1, keepdims=True))
            weights = jnp.exp2((scores - new[:, :1]) * (SCALE * LOG2E)).astype(BF16)
            shrink = jnp.exp2((old - new) * (SCALE * LOG2E))
            top[head] = new
            if waiting is not None:
                mix(*waiting)
            waiting = (head, weights, shrink)
            scores = following
        mix(*waiting)

    def teach(piece):
        def over(chunk, carry):
            attend(chunk, False)
            return carry

        lax.fori_loop(STEPS * piece, jnp.minimum(STEPS * (piece + 1), last), over, 0)

    sort(0)
    moments(0)
    others(CTX, me, lambda peer: q_copy(peer, peer).wait_recv())
    for head in range(HEADS):
        qh[head] = qr[:, :, head * DIM : (head + 1) * DIM].reshape(ROWS, DIM)
    for piece in range(1, PIECES):

        @pl.when(needs(chip, piece))
        def _(piece=piece):
            relay(piece)

    teach(0)
    for piece in range(1, PIECES):

        @pl.when(needs(chip, piece))
        def _(piece=piece):
            arrived(piece)
            sort(piece)
            moments(piece)
            teach(piece)

    attend(last, True)

    def close(head):
        total = acc[head]
        tq[head] = (total[:, :DIM] / total[:, DIM:]).astype(BF16)

    each(HEADS, close)

    for copy in weights:
        copy.wait()
    own_kv = kv[:, pl.ds(pl.multiple_of(HEAD_ROWS + SUB * me, SUB), SUB), :].reshape(ROWS, 2 * DIM)
    kown[...] = twice(own_kv[:, :DIM], 1)
    vown[...] = twice(own_kv[:, DIM:], 1)

    def forward(group):
        heads = [GROUP * group + index for index in range(GROUP)]
        mapped = [wide(nt(c_w[h], b_w[h]) * SCALE) for h in heads]
        read = [halves(nn(qh[h], m)) for h, m in zip(heads, mapped)]
        score = [nt(wide(r), kown[...]) for r in read]
        causal = place(iota((ROWS, ROWS), 1)) <= place(iota((ROWS, ROWS), 0))
        mixed = []
        for h, r, s in zip(heads, read, score):
            t_all[h] = r
            s_all[h] = s
            gap = twice(rcol[h], 1) - rows[0, pl.ds(h, 1), :]
            decay = jnp.where(causal, jnp.exp(gap), 0.0) * rows[1, pl.ds(h, 1), :]
            d_all[h] = decay
            high, low = split(s * decay)
            value = vown[:, :DIM]
            mixed.append(nn(high, value) + nn(low, value) + jnp.exp(rcol[h]) * product(r, mom[h]))
        flats = [nn(wide(m), twice(x_w[h], 0)) for h, m in zip(heads, mixed)]
        for h, m, flat in zip(heads, mixed, flats):
            z_all[h] = m
            y_all[h] = flat
            taught = tq[h].astype(F32)
            scaled = flat * gains[pl.ds(h, 1), :]
            stats[0] += flat * flat
            stats[1] += taught * taught
            stats[2] += scaled * scaled
            stats[3] += scaled * taught

    each(HEADS // GROUP, forward)

    lane = iota((ROWS, DIM), 1)
    packed = jnp.zeros((ROWS, DIM), F32)
    for index in range(4):
        packed = jnp.where(lane == index, jnp.sum(stats[index], axis=1, keepdims=True), packed)
    stx[tp] = packed.T[:8]

    def t_copy(peer, slot):
        return remote(stx.at[slot], stx.at[slot], t_ss.at[peer], t_rs.at[slot], {"tp": peer})

    others(TP, tp, lambda peer: t_copy(peer, tp).start())
    tangents(0)
    for piece in range(1, PIECES):

        @pl.when(needs(chip, piece))
        def _(piece=piece):
            tangents(piece)

    others(TP, tp, lambda peer: t_copy(peer, peer).wait_recv())
    sums = jnp.sum(stx[...], axis=0)
    inverse = lax.rsqrt(sums[0:1] / FEATURES + EPS)
    inverse_t = lax.rsqrt(sums[1:2] / FEATURES + EPS)
    cross = (2.0 / TOKENS) * (inverse * sums[2:3] - inverse_t * sums[3:4])
    pull = inverse * inverse * inverse * cross / FEATURES
    line = iota((8, ROWS), 0)
    spread = columns_of(jnp.where(line == 0, inverse, jnp.where(line == 1, inverse_t, pull)))
    for index in range(3):
        cols[index] = jnp.broadcast_to(spread[:, index : index + 1], (ROWS, DIM))

    def sib_copy(head):
        return remote(gbuf.at[1 - core, head], sibr.at[head], sib_ss.at[head], sib_rs.at[head], {"ctx": sibling})

    def r_copy(head, slot):
        return remote(pairsum.at[head], rs.at[slot], r_ss.at[head], r_rs.at[slot], {"ctx": 2 * head + core})

    def pass_on(group):
        for index in range(GROUP):
            head = GROUP * group + index
            sib_copy(head).wait_recv()
            pairsum[head] = gbuf[core, head] + sibr[head]

            @pl.when(head != chip)
            def _(head=head):
                r_copy(head, chip).start()

            @pl.when(head == chip)
            def _(head=head):
                rs[chip] = pairsum[head]

    def backward(group):
        heads = [GROUP * group + index for index in range(GROUP)]
        d_flats, small = [], []
        order = jnp.where(iota((ROWS, ROWS), 0) == place(iota((ROWS, ROWS), 1)), 1.0, 0.0).astype(BF16)
        for h in heads:
            flat = y_all[h]
            gain = gains[pl.ds(h, 1), :]
            inv = cols[0]
            unit = flat * inv
            normed = unit * gain
            out[:, pl.ds(pl.multiple_of(h * DIM, DIM), DIM)] = nn(order, normed.astype(BF16)).astype(BF16)
            d_normed = (2.0 / TOKENS) * (normed - tq[h].astype(F32) * cols[1])
            d_flat = d_normed * gain * inv - flat * cols[2]
            d_flats.append(d_flat)
            moved = d_flat * flat
            small.append([
                jnp.sum(d_normed * unit, axis=0, keepdims=True),
                jnp.sum(moved * rcol[h], axis=0, keepdims=True),
                jnp.sum(moved * rbcol[h], axis=0, keepdims=True),
            ])
        d_mixed = [nt(wide(d), twice(x_w[h], 1)) for h, d in zip(heads, d_flats)]
        d_score = [nt(wide(d), vown[...]) * d_all[h] for h, d in zip(heads, d_mixed)]
        for h, d in zip(heads, d_flats):
            gbuf[1, h, :DIM] = product(z_all[h].T, d)
        d_read = []
        for index, h in enumerate(heads):
            felt = jnp.sum(d_score[index] * s_all[h], axis=0, keepdims=True)
            from_decay = felt * rows[0, pl.ds(h, 1), :]
            from_bias = felt * (rows[3, pl.ds(h, 1), :] - rows[2, pl.ds(h, 1), :])
            high, low = split(d_score[index])
            key = kown[:, :DIM]
            d_late = jnp.exp(rcol[h]) * d_mixed[index]
            d_read.append(nn(high, key) + nn(low, key) + product_t(d_late, mom[h]))
            d_state = product(t_all[h].T, d_late)
            small[index][1] += jnp.sum(d_state * tangent[h, :DIM], axis=0, keepdims=True) - halves(from_decay)
            small[index][2] += jnp.sum(d_state * tangent[h, DIM:], axis=0, keepdims=True) + halves(from_bias)
        tail = iota((TAIL, DIM), 0)
        for index, h in enumerate(heads):
            query_t = qh[h].astype(F32).T.astype(BF16)
            gbuf[0, h, :DIM] = halves(nn(query_t, wide(d_read[index])))
            lines = jnp.zeros((TAIL, DIM), F32)
            for line, value in enumerate(small[index]):
                lines = jnp.where(tail == line, value, lines)
            gbuf[0, h, DIM:] = jnp.zeros((TAIL, DIM), F32)
            gbuf[1, h, DIM:] = lines
            sib_copy(h).start()

        @pl.when(group > 0)
        def _():
            pass_on(group - 1)

    each(HEADS // GROUP, backward)
    out_copy = pltpu.make_async_copy(out, out_to, out_sem.at[0])
    out_copy.start()
    pass_on(HEADS // GROUP - 1)

    others(CHIPS, chip, lambda peer: r_copy(peer, peer).wait_recv())
    fin[core, chip] = jnp.sum(rs[...], axis=0)

    def ag_copy(peer, slot):
        held = fin.at[core, slot]
        return remote(held, held, ag_ss.at[peer], ag_rs.at[slot], {"ctx": 2 * peer + core})

    def fw_copy(slot, side):
        held = fin.at[side, slot]
        return remote(held, held, fw_ss.at[slot], fw_rs.at[slot], {"ctx": sibling})

    others(CHIPS, chip, lambda peer: ag_copy(peer, chip).start())
    fw_copy(chip, core).start()

    def hand_over(peer):
        ag_copy(peer, peer).wait_recv()
        fw_copy(peer, core).start()

    others(CHIPS, chip, hand_over)
    for head in range(HEADS):
        fw_copy(head, 1 - core).wait_recv()
    fin_copy = pltpu.make_async_copy(fin, fin_to, out_sem.at[1])
    fin_copy.start()

    others(CTX, me, lambda peer: q_copy(peer, me).wait_send())
    for piece in range(PIECES):

        def left(peer, piece=piece):
            @pl.when(needs(peer, piece))
            def _():
                kv_copy(peer, chip, piece).wait_send()

        others(CHIPS, chip, left)

        @pl.when(needs(chip, piece))
        def _(piece=piece):
            for slot in range(CHIPS):
                kf_copy(slot, core, piece).wait_send()

    others(TP, tp, lambda peer: t_copy(peer, tp).wait_send())
    others(CHIPS, chip, lambda peer: r_copy(peer, chip).wait_send())
    others(CHIPS, chip, lambda peer: ag_copy(peer, chip).wait_send())
    for head in range(HEADS):
        sib_copy(head).wait_send()
        fw_copy(head, core).wait_send()
    out_copy.wait()
    fin_copy.wait()


def closing(out_in, fin, c_w, b_w, out, grad_c, grad_b, grad_x, grad_decay, grad_bias, grad_gain):
    out[...] = out_in[...]
    for head in range(HEADS):
        grad_x[head] = fin[1, head, :DIM]
        joint = fin[0, head, :DIM]
        grad_c[head] = nn(wide(joint), twice(b_w[head], 0)) * SCALE
        grad_b[head] = nn(wide(joint.T), twice(c_w[head], 0)) * SCALE
        grad_gain[head * DIM : (head + 1) * DIM] = fin[1, head, DIM]
        grad_decay[head] = jnp.sum(fin[1, head, DIM + 1])
        grad_bias[head] = jnp.sum(fin[1, head, DIM + 2])


def local(queries, keys, values, dt_logits, decay_log, dt_bias, c_weight, b_weight, x_weight, norm_gain):
    whole = pl.BlockSpec(memory_space=pltpu.VMEM)
    there = pl.BlockSpec(memory_space=pl.ANY)
    scalars = pl.BlockSpec(memory_space=pltpu.SMEM)
    dma = pltpu.SemaphoreType.DMA

    def f32(*shape):
        return pltpu.VMEM(shape, F32)

    def bf16(*shape):
        return pltpu.VMEM(shape, BF16)

    square = (HEADS, DIM, DIM)
    by_row = (HEADS, ROWS, DIM)
    message = (DIM + TAIL, DIM)
    out, fin = pl.pallas_call(
        kernel,
        out_shape=(
            jax.ShapeDtypeStruct((ROWS, HEADS * DIM), BF16),
            jax.ShapeDtypeStruct((2, HEADS, *message), F32),
        ),
        in_specs=[there] * 3 + [whole] + [scalars] * 2 + [there] * 3 + [whole],
        out_specs=[there] * 2,
        scratch_shapes=[
            bf16(CTX, SUB, HEADS * DIM),
            bf16(CTX, HEAD_ROWS + ROWS, 2 * DIM),
            bf16(CTX, ROWS, DIM),
            bf16(CTX, ROWS, 2 * DIM),
            bf16(*by_row),
            f32(ROWS, WIDTH * ROWS),
            f32(HEADS, ROWS, 2 * DIM),
            f32(*by_row),
            bf16(*by_row),
            f32(*square),
            f32(HEADS, 2 * DIM, DIM),
            f32(3, PIECES, HEADS, CTX * PIECE),
            f32(4, HEADS, ROWS),
            f32(*by_row),
            f32(*by_row),
            bf16(ROWS, 2 * DIM),
            bf16(ROWS, 2 * DIM),
            f32(HEADS, DIM),
            bf16(*square),
            bf16(*square),
            bf16(*square),
            f32(*by_row),
            f32(HEADS, ROWS, ROWS),
            f32(HEADS, ROWS, ROWS),
            f32(*by_row),
            f32(*by_row),
            f32(4, ROWS, DIM),
            f32(TP, 8, ROWS),
            f32(3, ROWS, DIM),
            bf16(ROWS, HEADS * DIM),
            f32(2, HEADS, *message),
            f32(HEADS, *message),
            f32(HEADS, *message),
            f32(CHIPS, *message),
            f32(2, HEADS, *message),
            dma((3,)), dma((3,)), dma((2,)),
            dma((CTX,)), dma((CTX,)),
            dma((CHIPS, PIECES)), dma((CHIPS, PIECES)), dma((CHIPS, PIECES)), dma((CHIPS, PIECES)),
            dma((TP,)), dma((TP,)),
            dma((HEADS,)), dma((HEADS,)), dma((CHIPS,)), dma((CHIPS,)),
            dma((CHIPS,)), dma((CHIPS,)), dma((HEADS,)), dma((HEADS,)),
        ],
        compiler_params=pltpu.CompilerParams(
            collective_id=0, has_side_effects=True, vmem_limit_bytes=56 * 2**20
        ),
    )(queries, keys, values, dt_logits, decay_log, dt_bias, c_weight, b_weight, x_weight, norm_gain)
    return pl.pallas_call(
        closing,
        out_shape=(
            jax.ShapeDtypeStruct((ROWS, HEADS * DIM), BF16),
            jax.ShapeDtypeStruct(square, F32),
            jax.ShapeDtypeStruct(square, F32),
            jax.ShapeDtypeStruct(square, F32),
            jax.ShapeDtypeStruct((HEADS,), F32),
            jax.ShapeDtypeStruct((HEADS,), F32),
            jax.ShapeDtypeStruct((HEADS * DIM,), F32),
        ),
        in_specs=[whole] * 4,
        out_specs=[whole] * 4 + [scalars] * 2 + [whole],
        compiler_params=pltpu.CompilerParams(vmem_limit_bytes=32 * 2**20),
    )(out, fin, c_weight, b_weight)


def solution(mesh):
    return jax.shard_map(
        local,
        mesh=mesh,
        in_specs=(
            P("ctx", "tp"),
            P("ctx", "tp"),
            P("ctx", "tp"),
            P("ctx", "tp"),
            P("tp"),
            P("tp"),
            P("tp", None, None),
            P("tp", None, None),
            P("tp", None, None),
            P("tp"),
        ),
        out_specs=(
            P("ctx", "tp"),
            P("tp", None, None),
            P("tp", None, None),
            P("tp", None, None),
            P("tp"),
            P("tp"),
            P("tp"),
        ),
        check_vma=False,
    )
```

time: 130 us -> 86.9 us (0.67)
  Pallas kernels: 118 us -> 82 us
  local copies, waits for them, and re-layouts: 9.93 us -> 3.77 us
    pallas_call x1, Pallas kernels: 118 us -> 80.2 us  [local(): pl.pallas_call(kernel, out_shape=(jax.ShapeDtypeStruct((ROWS, HEADS * DIM...]
    unnamed x16 -> x9, local copies, waits for them, and re-layouts: 6.5 us -> 3.77 us
    reshape x3 -> x0, local copies, waits for them, and re-layouts: 1.94 us -> none  [the longest x1 0.67 us: local(): decay_log.reshape(HEADS, 1)]
    pallas_call x0 -> x1, Pallas kernels: none -> 1.76 us  [local(): pl.pallas_call(closing, out_shape=(jax.ShapeDtypeStruct((ROWS, HEADS * DI...]
    slice x1 -> x0, local copies, waits for them, and re-layouts: 1.5 us -> none  [local(): small[HEADS:, 1]]
where the time goes in v2:
time: 86.9 us; the launch traced here: 86.6 us
  Pallas kernels  82 us (94%)
  local copies, waits for them, and re-layouts  3.77 us (4%)
    pallas_call x1, Pallas kernels, local(): pl.pallas_call(kernel, out_shape=(jax.ShapeDtypeStruct((ROWS, HEADS * DIM...  80.2 us
    unnamed x9, local copies, waits for them, and re-layouts  3.77 us
    pallas_call x1, Pallas kernels, local(): pl.pallas_call(closing, out_shape=(jax.ShapeDtypeStruct((ROWS, HEADS * DI...  1.76 us

profile of v2, /device:TPU:1, one launch (start us, length us, event | category | flops | bytes accessed | tf_op | source)
XLA Modules:
  0.0 86.6 jit_solution(12633908582240598572)
XLA Ops:
  0.6 0.0 copy-start.2
  0.6 0.0 copy-start.1
  0.7 1.5 %copy.17.z_in = bf16[256,8]{1,0:T(8,128)(2,1)} copy(bf16[256,8]{0,1:T(8,128)(2,1)} %param.13) | data formatting | bytes 8192 | tf_op args[3]
  2.1 80.2 %shard_map.153 = (bf16[256,1024]{1,0:T(8,128)(2,1)}, f32[2,8,136,128]{3,2,1,0:T(8,128)}) custom-call(bf16[256,1024]{1,0:T(8,128)(2,1)} %q_in.1, bf16[256,128]{1,0:T(8,128)(2,1)} %k_in.1, bf16[256,128]{1,0:T(8,128)(2,1)} %v_in.1, bf16[256,8]{1,0:T(8,128)(2,1)} %copy.17.z_in, f32[8]{0:T(128)} %decay_in.1, f32[8]{0:T(128)} %bias_in.1, ...), custom_call_target="tpu_custom_call" | custom-call | tf_op jit(solution)/shard_map/pallas_call | solution.py:573
  82.4 0.0 copy-done.2
  82.4 0.0 copy-done.1
  82.4 0.0 copy-start
  82.4 1.2 %copy-done = f32[2,8,136,128]{3,2,1,0:T(8,128)S(1)} copy-done((f32[2,8,136,128]{3,2,1,0:T(8,128)S(1)}, f32[2,8,136,128]{3,2,1,0:T(8,128)}, u32[]{:S(2)}) %copy-start) | copy-done | bytes 1114136
  83.6 0.0 copy-start.3
  83.6 1.0 %copy-done.3 = bf16[256,1024]{1,0:T(8,128)(2,1)S(1)} copy-done((bf16[256,1024]{1,0:T(8,128)(2,1)S(1)}, bf16[256,1024]{1,0:T(8,128)(2,1)}, u32[]{:S(2)}) %copy-start.3) | copy-done | bytes 524312
  84.7 1.8 %shard_map.154 = (bf16[256,1024]{1,0:T(8,128)(2,1)}, f32[8,128,128]{2,1,0:T(8,128)}, f32[8,128,128]{2,1,0:T(8,128)}, f32[8,128,128]{2,1,0:T(8,128)}, f32[8]{0:T(128)}, /*index=5*/f32[8]{0:T(128)}, f32[1024]{0:T(1024)}) custom-call(bf16[256,1024]{1,0:T(8,128)(2,1)S(1)} %copy-done.3, f32[2,8,136,128]{3,2,1,0:T(8,128)S(1)} %copy-done, ...), custom_call_target="tpu_custom_call" | custom-call | tf_op jit(solution)/shard_map/pallas_call | solution.py:628
Async XLA Ops:
  0.6 81.7 %copy-start.2 = (bf16[8,128,128]{2,1,0:T(8,128)(2,1)S(1)}, bf16[8,128,128]{2,1,0:T(8,128)(2,1)}, u32[]{:S(2)}) copy-start(bf16[8,128,128]{2,1,0:T(8,128)(2,1)} %b_w.1) | copy-start | bytes 786436
  0.6 81.7 %copy-start.1 = (bf16[8,128,128]{2,1,0:T(8,128)(2,1)S(1)}, bf16[8,128,128]{2,1,0:T(8,128)(2,1)}, u32[]{:S(2)}) copy-start(bf16[8,128,128]{2,1,0:T(8,128)(2,1)} %c_w.1) | copy-start | bytes 786436
  82.4 1.2 %copy-start = (f32[2,8,136,128]{3,2,1,0:T(8,128)S(1)}, f32[2,8,136,128]{3,2,1,0:T(8,128)}, u32[]{:S(2)}) copy-start(f32[2,8,136,128]{3,2,1,0:T(8,128)} %get-tuple-element.10.fin) | copy-start | bytes 3342340
  83.6 1.0 %copy-start.3 = (bf16[256,1024]{1,0:T(8,128)(2,1)S(1)}, bf16[256,1024]{1,0:T(8,128)(2,1)}, u32[]{:S(2)}) copy-start(bf16[256,1024]{1,0:T(8,128)(2,1)} %get-tuple-element.9.out_in) | copy-start | bytes 1572868

commit v3 on v2

--- a/solution.py
+++ b/solution.py
@@ -29,6 +29,7 @@
 SCALE = DIM**-0.5
 LOG2E = 1.4426950408889634
 NEG = -1e30
+ORDER = (0, 2, 5, 7, 1, 3, 4, 6)
 
 
 def nn(a, b):
@@ -97,12 +98,13 @@
 
 
 def kernel(
-    q_in, k_in, v_in, z_in, decay_in, bias_in, c_in, b_in, x_in, gain_in,
+    q_in, k_in, v_in, z_hbm, decay_hbm, bias_hbm, c_in, b_in, x_in, gain_hbm,
     out_to, fin_to,
-    qr, kv, kpos, vpos, qh, hide, acc, top, tq, mom, tangent, wts, rows, rcol, rbcol, kown, vown, gains,
+    qr, kv, kpos, vpos, qh, hide, acc, top, tq, mom, tangent, wts, rows, rcol, rbcol, kown, vown, gains, both_maps,
     c_w, b_w, x_w, t_all, s_all, d_all, z_all, y_all, stats, stx, cols, out,
     gbuf, sibr, pairsum, rs, fin,
-    local_sem, w_sem, out_sem, q_ss, q_rs, kv_ss, kv_rs, kf_ss, kf_rs, t_ss, t_rs, sib_ss, sib_rs, r_ss, r_rs,
+    z_in, decay_in, bias_in, gain_in,
+    local_sem, w_sem, out_sem, fin_sem, q_ss, q_rs, kv_ss, kv_rs, kf_ss, kf_rs, t_ss, t_rs, sib_ss, sib_rs, r_ss, r_rs,
     ag_ss, ag_rs, fw_ss, fw_rs,
 ):
     me = lax.axis_index("ctx")
@@ -134,6 +136,14 @@
         pltpu.make_async_copy(v_in, kv.at[me, body_rows, pl.ds(DIM, DIM)], local_sem.at[1]),
         pltpu.make_async_copy(q_in.at[own_rows], qr.at[me], local_sem.at[2]),
     ]
+    few = [
+        pltpu.make_async_copy(z_hbm, z_in, local_sem.at[3]),
+        pltpu.make_async_copy(decay_hbm, decay_in, local_sem.at[4]),
+        pltpu.make_async_copy(bias_hbm, bias_in, local_sem.at[5]),
+        pltpu.make_async_copy(gain_hbm, gain_in, local_sem.at[6]),
+    ]
+    for copy in few:
+        copy.start()
     for copy in own:
         copy.start()
     weights = [
@@ -146,60 +156,10 @@
     barrier = pltpu.get_barrier_semaphore()
     others(CTX, me, lambda peer: pl.semaphore_signal(barrier, inc=1, device_id={"ctx": peer}, device_id_type=MESH))
     others(TP, tp, lambda peer: pl.semaphore_signal(barrier, inc=1, device_id={"tp": peer}, device_id_type=MESH))
-    turn = jnp.where(iota((HEAD_ROWS, HEADS), 0) == iota((HEAD_ROWS, HEADS), 1), 1.0, 0.0).astype(BF16)
-    kv[me, :HEAD_ROWS, :] = nt(turn, z_in[...]).astype(BF16)
-    for copy in own:
+    for copy in few:
         copy.wait()
-    pl.semaphore_wait(barrier, CTX - 1 + TP - 1)
-
-    def part_of(piece):
-        if piece == 0:
-            return pl.ds(0, HEAD_ROWS + PIECE)
-        return pl.ds(HEAD_ROWS + PIECE * piece, PIECE)
-
-    def kv_copy(peer, slot, piece):
-        held = kv.at[2 * slot + core, part_of(piece)]
-        return remote(held, held, kv_ss.at[peer, piece], kv_rs.at[slot, piece], {"ctx": 2 * peer + core})
-
-    def kf_copy(slot, side, piece):
-        held = kv.at[2 * slot + side, part_of(piece)]
-        return remote(held, held, kf_ss.at[slot, piece], kf_rs.at[slot, piece], {"ctx": sibling})
-
-    def needs(peer, piece):
-        return peer >= piece * (CHIPS // PIECES)
-
-    def q_copy(peer, slot):
-        taken = pl.ds(pl.multiple_of(SUB * peer, SUB), SUB)
-        return remote(q_in.at[taken], qr.at[slot], q_ss.at[peer], q_rs.at[slot], {"ctx": peer})
-
-    def send_piece(piece):
-        def send(peer):
-            @pl.when(needs(peer, piece))
-            def _():
-                kv_copy(peer, chip, piece).start()
-
-        others(CHIPS, chip, send)
-
-        @pl.when(needs(chip, piece))
-        def _():
-            kf_copy(chip, core, piece).start()
-
-    def relay(piece):
-        def one(peer):
-            kv_copy(peer, peer, piece).wait_recv()
-            kf_copy(peer, core, piece).start()
-
-        others(CHIPS, chip, one)
-
-    def arrived(piece):
-        kf_copy(chip, 1 - core, piece).wait_recv()
-        others(CHIPS, chip, lambda peer: kf_copy(peer, 1 - core, piece).wait_recv())
-
-    send_piece(0)
-    others(CTX, me, lambda peer: q_copy(peer, me).start())
-    for piece in range(1, PIECES):
-        send_piece(piece)
-
+    own_z = z_in[...].astype(F32)
+    kv[me, :HEAD_ROWS, :] = jnp.concatenate([own_z, jnp.zeros_like(own_z)], axis=0).astype(BF16)
     for head in range(HEADS):
         gains[head : head + 1, :] = gain_in[head * DIM : (head + 1) * DIM].reshape(1, DIM)
         acc[head] = jnp.zeros((ROWS, 2 * DIM), F32)
@@ -218,6 +178,62 @@
         decay_rate = jnp.where(head_line == head, decay_in[head], decay_rate)
         bias = jnp.where(head_line == head, bias_in[head], bias)
     speed = -jnp.exp(decay_rate)
+    for copy in weights[:2]:
+        copy.wait()
+    for head in range(HEADS):
+        both_maps[head] = wide(nt(c_w[head], b_w[head]) * SCALE)
+    for copy in own:
+        copy.wait()
+    pl.semaphore_wait(barrier, CTX - 1 + TP - 1)
+
+    def part_of(piece):
+        if piece == 0:
+            return pl.ds(0, HEAD_ROWS + PIECE)
+        return pl.ds(HEAD_ROWS + PIECE * piece, PIECE)
+
+    def kv_copy(peer, slot, piece):
+        held = kv.at[2 * slot + core, part_of(piece)]
+        return remote(held, held, kv_ss.at[peer, piece], kv_rs.at[slot, piece], {"ctx": 2 * peer + core})
+
+    def kf_copy(slot, side, piece):
+        held = kv.at[2 * slot + side, part_of(piece)]
+        return remote(held, held, kf_ss.at[slot, piece], kf_rs.at[slot, piece], {"ctx": sibling})
+
+    def needs(peer, piece):
+        return peer >= piece * (CHIPS // PIECES)
+
+    def q_copy(peer, slot):
+        taken = pl.ds(pl.multiple_of(SUB * peer, SUB), SUB)
+        return remote(q_in.at[taken], qr.at[slot], q_ss.at[peer], q_rs.at[slot], {"ctx": peer})
+
+    def send_piece(piece):
+        def send(peer):
+            @pl.when(needs(peer, piece))
+            def _():
+                kv_copy(peer, chip, piece).start()
+
+        others(CHIPS, chip, send)
+
+        @pl.when(needs(chip, piece))
+        def _():
+            kf_copy(chip, core, piece).start()
+
+    def relay(piece):
+        def one(peer):
+            kv_copy(peer, peer, piece).wait_recv()
+            kf_copy(peer, core, piece).start()
+
+        others(CHIPS, chip, one)
+
+    def arrived(piece):
+        kf_copy(chip, 1 - core, piece).wait_recv()
+        others(CHIPS, chip, lambda peer: kf_copy(peer, 1 - core, piece).wait_recv())
+
+    send_piece(0)
+    others(CTX, me, lambda peer: q_copy(peer, me).start())
+    for piece in range(1, PIECES):
+        send_piece(piece)
+
     relay(0)
     arrived(0)
 
@@ -319,34 +335,29 @@
             scores = following
         mix(*waiting)
 
-    def teach(piece):
-        def over(chunk, carry):
-            attend(chunk, False)
-            return carry
-
-        lax.fori_loop(STEPS * piece, jnp.minimum(STEPS * (piece + 1), last), over, 0)
-
     sort(0)
     moments(0)
     others(CTX, me, lambda peer: q_copy(peer, peer).wait_recv())
     for head in range(HEADS):
         qh[head] = qr[:, :, head * DIM : (head + 1) * DIM].reshape(ROWS, DIM)
-    for piece in range(1, PIECES):
-
-        @pl.when(needs(chip, piece))
-        def _(piece=piece):
-            relay(piece)
-
-    teach(0)
-    for piece in range(1, PIECES):
-
-        @pl.when(needs(chip, piece))
-        def _(piece=piece):
-            arrived(piece)
-            sort(piece)
-            moments(piece)
-            teach(piece)
-
+
+    def teach(chunk, carry):
+        attend(chunk, False)
+        for piece in range(1, PIECES):
+
+            @pl.when(needs(chip, piece) & (chunk == STEPS * piece - 2))
+            def _(piece=piece):
+                relay(piece)
+
+            @pl.when(needs(chip, piece) & (chunk == STEPS * piece - 1))
+            def _(piece=piece):
+                arrived(piece)
+                sort(piece)
+                moments(piece)
+
+        return carry
+
+    lax.fori_loop(0, last, teach, 0)
     attend(last, True)
 
     def close(head):
@@ -355,16 +366,14 @@
 
     each(HEADS, close)
 
-    for copy in weights:
-        copy.wait()
+    weights[2].wait()
     own_kv = kv[:, pl.ds(pl.multiple_of(HEAD_ROWS + SUB * me, SUB), SUB), :].reshape(ROWS, 2 * DIM)
     kown[...] = twice(own_kv[:, :DIM], 1)
     vown[...] = twice(own_kv[:, DIM:], 1)
 
     def forward(group):
         heads = [GROUP * group + index for index in range(GROUP)]
-        mapped = [wide(nt(c_w[h], b_w[h]) * SCALE) for h in heads]
-        read = [halves(nn(qh[h], m)) for h, m in zip(heads, mapped)]
+        read = [halves(nn(qh[h], both_maps[h])) for h in heads]
         score = [nt(wide(r), kown[...]) for r in read]
         causal = place(iota((ROWS, ROWS), 1)) <= place(iota((ROWS, ROWS), 0))
         mixed = []
@@ -418,28 +427,44 @@
     for index in range(3):
         cols[index] = jnp.broadcast_to(spread[:, index : index + 1], (ROWS, DIM))
 
-    def sib_copy(head):
-        return remote(gbuf.at[1 - core, head], sibr.at[head], sib_ss.at[head], sib_rs.at[head], {"ctx": sibling})
-
-    def r_copy(head, slot):
-        return remote(pairsum.at[head], rs.at[slot], r_ss.at[head], r_rs.at[slot], {"ctx": 2 * head + core})
+    def sib_copy(group):
+        part = pl.ds(GROUP * group, GROUP)
+        return remote(gbuf.at[1 - core, part], sibr.at[part], sib_ss.at[group], sib_rs.at[group], {"ctx": sibling})
+
+    def r_copy(turn, head, slot):
+        return remote(pairsum.at[turn], rs.at[slot], r_ss.at[head], r_rs.at[slot], {"ctx": 2 * head + core})
+
+    def turns(group):
+        heads = []
+        for index in range(GROUP):
+            turn = GROUP * group + index
+            owner = (chip + turn) & 3
+            first = (owner >> 1) * 5 + (owner & 1) * 2
+            heads.append(jnp.where(turn < HEADS // 2, first, first + 1 - 2 * (first & 1)))
+        return heads
+
+    def order_of(head):
+        if isinstance(head, int):
+            return ORDER.index(head)
+        late = (head + (head >> 2)) & 1
+        return 4 * late + 2 * (head >> 2) + ((head & 3) >> 1)
 
     def pass_on(group):
-        for index in range(GROUP):
-            head = GROUP * group + index
-            sib_copy(head).wait_recv()
-            pairsum[head] = gbuf[core, head] + sibr[head]
+        sib_copy(group).wait_recv()
+        for index, head in enumerate(turns(group)):
+            turn = GROUP * group + index
+            pairsum[turn] = gbuf[core, turn] + sibr[turn]
 
             @pl.when(head != chip)
-            def _(head=head):
-                r_copy(head, chip).start()
+            def _(head=head, turn=turn):
+                r_copy(turn, head, chip).start()
 
             @pl.when(head == chip)
-            def _(head=head):
-                rs[chip] = pairsum[head]
+            def _(turn=turn):
+                rs[chip] = pairsum[turn]
 
     def backward(group):
-        heads = [GROUP * group + index for index in range(GROUP)]
+        heads = turns(group)
         d_flats, small = [], []
         order = jnp.where(iota((ROWS, ROWS), 0) == place(iota((ROWS, ROWS), 1)), 1.0, 0.0).astype(BF16)
         for h in heads:
@@ -460,8 +485,8 @@
             ])
         d_mixed = [nt(wide(d), twice(x_w[h], 1)) for h, d in zip(heads, d_flats)]
         d_score = [nt(wide(d), vown[...]) * d_all[h] for h, d in zip(heads, d_mixed)]
-        for h, d in zip(heads, d_flats):
-            gbuf[1, h, :DIM] = product(z_all[h].T, d)
+        for index, h in enumerate(heads):
+            gbuf[1, GROUP * group + index, :DIM] = product(z_all[h].T, d_flats[index])
         d_read = []
         for index, h in enumerate(heads):
             felt = jnp.sum(d_score[index] * s_all[h], axis=0, keepdims=True)
@@ -477,13 +502,14 @@
         tail = iota((TAIL, DIM), 0)
         for index, h in enumerate(heads):
             query_t = qh[h].astype(F32).T.astype(BF16)
-            gbuf[0, h, :DIM] = halves(nn(query_t, wide(d_read[index])))
+            turn = GROUP * group + index
+            gbuf[0, turn, :DIM] = halves(nn(query_t, wide(d_read[index])))
             lines = jnp.zeros((TAIL, DIM), F32)
             for line, value in enumerate(small[index]):
                 lines = jnp.where(tail == line, value, lines)
-            gbuf[0, h, DIM:] = jnp.zeros((TAIL, DIM), F32)
-            gbuf[1, h, DIM:] = lines
-            sib_copy(h).start()
+            gbuf[0, turn, DIM:] = jnp.zeros((TAIL, DIM), F32)
+            gbuf[1, turn, DIM:] = lines
+        sib_copy(group).start()
 
         @pl.when(group > 0)
         def _():
@@ -494,29 +520,33 @@
     out_copy.start()
     pass_on(HEADS // GROUP - 1)
 
-    others(CHIPS, chip, lambda peer: r_copy(peer, peer).wait_recv())
-    fin[core, chip] = jnp.sum(rs[...], axis=0)
+    others(CHIPS, chip, lambda peer: r_copy(0, peer, peer).wait_recv())
+    fin[core, order_of(chip)] = jnp.sum(rs[...], axis=0)
 
     def ag_copy(peer, slot):
-        held = fin.at[core, slot]
+        held = fin.at[core, order_of(slot)]
         return remote(held, held, ag_ss.at[peer], ag_rs.at[slot], {"ctx": 2 * peer + core})
 
-    def fw_copy(slot, side):
-        held = fin.at[side, slot]
-        return remote(held, held, fw_ss.at[slot], fw_rs.at[slot], {"ctx": sibling})
+    def fw_copy(half, side):
+        held = fin.at[side, pl.ds(half * (CHIPS // 2), CHIPS // 2)]
+        return remote(held, held, fw_ss.at[half], fw_rs.at[half], {"ctx": sibling})
+
+    def fin_copy(half):
+        part = pl.ds(half * (CHIPS // 2), CHIPS // 2)
+        return pltpu.make_async_copy(fin.at[:, part], fin_to.at[:, part], fin_sem.at[half])
 
     others(CHIPS, chip, lambda peer: ag_copy(peer, chip).start())
-    fw_copy(chip, core).start()
-
-    def hand_over(peer):
-        ag_copy(peer, peer).wait_recv()
-        fw_copy(peer, core).start()
-
-    others(CHIPS, chip, hand_over)
-    for head in range(HEADS):
-        fw_copy(head, 1 - core).wait_recv()
-    fin_copy = pltpu.make_async_copy(fin, fin_to, out_sem.at[1])
-    fin_copy.start()
+    for half in range(2):
+        for head in ORDER[half * (CHIPS // 2) : (half + 1) * (CHIPS // 2)]:
+
+            @pl.when(chip != head)
+            def _(head=head):
+                ag_copy(head, head).wait_recv()
+
+        fw_copy(half, core).start()
+    for half in range(2):
+        fw_copy(half, 1 - core).wait_recv()
+        fin_copy(half).start()
 
     others(CTX, me, lambda peer: q_copy(peer, me).wait_send())
     for piece in range(PIECES):
@@ -534,25 +564,27 @@
                 kf_copy(slot, core, piece).wait_send()
 
     others(TP, tp, lambda peer: t_copy(peer, tp).wait_send())
-    others(CHIPS, chip, lambda peer: r_copy(peer, chip).wait_send())
+    others(CHIPS, chip, lambda peer: r_copy(0, peer, chip).wait_send())
     others(CHIPS, chip, lambda peer: ag_copy(peer, chip).wait_send())
-    for head in range(HEADS):
-        sib_copy(head).wait_send()
-        fw_copy(head, core).wait_send()
+    for group in range(HEADS // GROUP):
+        sib_copy(group).wait_send()
+    for half in range(2):
+        fw_copy(half, core).wait_send()
+        fin_copy(half).wait()
     out_copy.wait()
-    fin_copy.wait()
 
 
 def closing(out_in, fin, c_w, b_w, out, grad_c, grad_b, grad_x, grad_decay, grad_bias, grad_gain):
     out[...] = out_in[...]
     for head in range(HEADS):
-        grad_x[head] = fin[1, head, :DIM]
-        joint = fin[0, head, :DIM]
+        slot = ORDER.index(head)
+        grad_x[head] = fin[1, slot, :DIM]
+        joint = fin[0, slot, :DIM]
         grad_c[head] = nn(wide(joint), twice(b_w[head], 0)) * SCALE
         grad_b[head] = nn(wide(joint.T), twice(c_w[head], 0)) * SCALE
-        grad_gain[head * DIM : (head + 1) * DIM] = fin[1, head, DIM]
-        grad_decay[head] = jnp.sum(fin[1, head, DIM + 1])
-        grad_bias[head] = jnp.sum(fin[1, head, DIM + 2])
+        grad_gain[head * DIM : (head + 1) * DIM] = fin[1, slot, DIM]
+        grad_decay[head] = jnp.sum(fin[1, slot, DIM + 1])
+        grad_bias[head] = jnp.sum(fin[1, slot, DIM + 2])
 
 
 def local(queries, keys, values, dt_logits, decay_log, dt_bias, c_weight, b_weight, x_weight, norm_gain):
@@ -570,13 +602,17 @@
     square = (HEADS, DIM, DIM)
     by_row = (HEADS, ROWS, DIM)
     message = (DIM + TAIL, DIM)
+    arguments = (
+        queries, keys, values, dt_logits.T, decay_log, dt_bias, c_weight, b_weight, x_weight, norm_gain,
+    )
+    given = [pltpu.with_memory_space_constraint(a, pltpu.HBM) for a in arguments]
     out, fin = pl.pallas_call(
         kernel,
         out_shape=(
             jax.ShapeDtypeStruct((ROWS, HEADS * DIM), BF16),
             jax.ShapeDtypeStruct((2, HEADS, *message), F32),
         ),
-        in_specs=[there] * 3 + [whole] + [scalars] * 2 + [there] * 3 + [whole],
+        in_specs=[pl.BlockSpec(memory_space=pltpu.HBM)] * 10,
         out_specs=[there] * 2,
         scratch_shapes=[
             bf16(CTX, SUB, HEADS * DIM),
@@ -597,6 +633,7 @@
             bf16(ROWS, 2 * DIM),
             bf16(ROWS, 2 * DIM),
             f32(HEADS, DIM),
+            bf16(HEADS, DIM, 2 * DIM),
             bf16(*square),
             bf16(*square),
             bf16(*square),
@@ -614,17 +651,21 @@
             f32(HEADS, *message),
             f32(CHIPS, *message),
             f32(2, HEADS, *message),
-            dma((3,)), dma((3,)), dma((2,)),
+            bf16(HEADS, ROWS),
+            pltpu.SMEM((HEADS,), F32),
+            pltpu.SMEM((HEADS,), F32),
+            f32(HEADS * DIM),
+            dma((7,)), dma((3,)), dma((1,)), dma((2,)),
             dma((CTX,)), dma((CTX,)),
             dma((CHIPS, PIECES)), dma((CHIPS, PIECES)), dma((CHIPS, PIECES)), dma((CHIPS, PIECES)),
             dma((TP,)), dma((TP,)),
-            dma((HEADS,)), dma((HEADS,)), dma((CHIPS,)), dma((CHIPS,)),
-            dma((CHIPS,)), dma((CHIPS,)), dma((HEADS,)), dma((HEADS,)),
+            dma((HEADS // GROUP,)), dma((HEADS // GROUP,)), dma((CHIPS,)), dma((CHIPS,)),
+            dma((CHIPS,)), dma((CHIPS,)), dma((2,)), dma((2,)),
         ],
         compiler_params=pltpu.CompilerParams(
-            collective_id=0, has_side_effects=True, vmem_limit_bytes=56 * 2**20
+            collective_id=0, has_side_effects=True, vmem_limit_bytes=40 * 2**20
         ),
-    )(queries, keys, values, dt_logits, decay_log, dt_bias, c_weight, b_weight, x_weight, norm_gain)
+    )(*given)
     return pl.pallas_call(
         closing,
         out_shape=(
@@ -638,7 +679,7 @@
         ),
         in_specs=[whole] * 4,
         out_specs=[whole] * 4 + [scalars] * 2 + [whole],
-        compiler_params=pltpu.CompilerParams(vmem_limit_bytes=32 * 2**20),
+        compiler_params=pltpu.CompilerParams(vmem_limit_bytes=16 * 2**20),
     )(out, fin, c_weight, b_weight)
 
 

time: 86.9 us -> 77.6 us (0.89)
  Pallas kernels: 82 us -> 76.6 us
  local copies, waits for them, and re-layouts: 3.77 us -> 0.01 us
    pallas_call x1, Pallas kernels: 80.2 us -> 74.9 us  [local(): pl.pallas_call(kernel, out_shape=(jax.ShapeDtypeStruct((ROWS, HEADS * DIM...]
    unnamed x9 -> x4, local copies, waits for them, and re-layouts: 3.77 us -> 0.01 us
where the time goes in v3:
time: 77.6 us; the launch traced here: 77.5 us
  Pallas kernels  76.6 us (99%)
  between operations  0.84 us (1%)
    pallas_call x1, Pallas kernels, local(): pl.pallas_call(kernel, out_shape=(jax.ShapeDtypeStruct((ROWS, HEADS * DIM...  74.9 us
    pallas_call x1, Pallas kernels, local(): pl.pallas_call(closing, out_shape=(jax.ShapeDtypeStruct((ROWS, HEADS * DI...  1.76 us

profile of v3, /device:TPU:1, one launch (start us, length us, event | category | flops | bytes accessed | tf_op | source)
XLA Modules:
  0.0 77.5 jit_solution(11139966269099943341)
XLA Ops:
  0.6 0.0 copy-start.1
  0.6 0.0 copy-start
  0.7 74.9 %shard_map.153 = (bf16[256,1024]{1,0:T(8,128)(2,1)S(1)}, f32[2,8,136,128]{3,2,1,0:T(8,128)S(1)}) custom-call(bf16[256,1024]{1,0:T(8,128)(2,1)} %q_in.1, bf16[256,128]{1,0:T(8,128)(2,1)} %k_in.1, bf16[256,128]{1,0:T(8,128)(2,1)} %v_in.1, bf16[8,256]{1,0:T(8,128)(2,1)} %bitcast.1, f32[8]{0:T(128)} %decay_hbm.1, f32[8]{0:T(128)} %bias_hbm.1, ...), custom_call_target="tpu_custom_call" | custom-call | tf_op jit(solution)/shard_map/pallas_call | solution.py:609
  75.5 0.0 copy-done.1
  75.6 0.0 copy-done
  75.6 1.8 %shard_map.154 = (bf16[256,1024]{1,0:T(8,128)(2,1)}, f32[8,128,128]{2,1,0:T(8,128)}, f32[8,128,128]{2,1,0:T(8,128)}, f32[8,128,128]{2,1,0:T(8,128)}, f32[8]{0:T(128)}, /*index=5*/f32[8]{0:T(128)}, f32[1024]{0:T(1024)}) custom-call(bf16[256,1024]{1,0:T(8,128)(2,1)S(1)} %get-tuple-element.9.out_in, f32[2,8,136,128]{3,2,1,0:T(8,128)S(1)} %get-tuple-element.10.fin, ...), custom_call_target="tpu_custom_call" | custom-call | tf_op jit(solution)/shard_map/pallas_call | solution.py:669
Async XLA Ops:
  0.6 74.9 %copy-start.1 = (bf16[8,128,128]{2,1,0:T(8,128)(2,1)S(1)}, bf16[8,128,128]{2,1,0:T(8,128)(2,1)}, u32[]{:S(2)}) copy-start(bf16[8,128,128]{2,1,0:T(8,128)(2,1)} %b_w.1) | copy-start | bytes 786436
  0.6 74.9 %copy-start = (bf16[8,128,128]{2,1,0:T(8,128)(2,1)S(1)}, bf16[8,128,128]{2,1,0:T(8,128)(2,1)}, u32[]{:S(2)}) copy-start(bf16[8,128,128]{2,1,0:T(8,128)(2,1)} %c_w.1) | copy-start | bytes 786436

commit v4 on v3

--- a/solution.py
+++ b/solution.py
@@ -15,14 +15,15 @@
 TP = 8
 CHIPS = CTX // 2
 SUB = ROWS // CTX
-PIECES = 2
-PIECE = ROWS // PIECES
+STARTS = (0, 64, 128)
+SIZES = (64, 64, 128)
+PIECES = len(STARTS)
 WIDTH = 4
-STEPS = CTX // PIECES // WIDTH
-QUAD = 4
+KEYS = 512
 HEAD_ROWS = 16
 TAIL = 8
 GROUP = 2
+FORWARD = 4
 TOKENS = ROWS * CTX
 FEATURES = HEADS * DIM * TP
 EPS = 1e-05
@@ -188,8 +189,8 @@
 
     def part_of(piece):
         if piece == 0:
-            return pl.ds(0, HEAD_ROWS + PIECE)
-        return pl.ds(HEAD_ROWS + PIECE * piece, PIECE)
+            return pl.ds(0, HEAD_ROWS + SIZES[0])
+        return pl.ds(HEAD_ROWS + STARTS[piece], SIZES[piece])
 
     def kv_copy(peer, slot, piece):
         held = kv.at[2 * slot + core, part_of(piece)]
@@ -200,7 +201,7 @@
         return remote(held, held, kf_ss.at[slot, piece], kf_rs.at[slot, piece], {"ctx": sibling})
 
     def needs(peer, piece):
-        return peer >= piece * (CHIPS // PIECES)
+        return peer >= STARTS[piece] // SUB // 2
 
     def q_copy(peer, slot):
         taken = pl.ds(pl.multiple_of(SUB * peer, SUB), SUB)
@@ -251,8 +252,9 @@
         weight = jnp.where(earlier, jnp.exp(span) * step[source], 0.0)
         kinds = (weight, weight * span, weight * (span_b + slope[source] / step[source]))
         for index, kind in enumerate(kinds):
-            for piece in range(PIECES):
-                wts[index, piece, :, source * PIECE : (source + 1) * PIECE] = kind[:, piece * PIECE : (piece + 1) * PIECE]
+            for start, size in zip(STARTS, SIZES):
+                at = CTX * start + source * size
+                wts[index, :, at : at + size] = kind[:, start : start + size]
         span = span + rate[source]
         span_b = span_b + rate_b[source]
 
@@ -274,41 +276,42 @@
         rcol[head] = jnp.broadcast_to(running_c[:, head : head + 1], (ROWS, DIM))
         rbcol[head] = jnp.broadcast_to(running_bc[:, head : head + 1], (ROWS, DIM))
 
-    def gathered(piece, quad):
-        part = kv[pl.ds(QUAD * quad, QUAD), pl.ds(HEAD_ROWS + PIECE * piece, PIECE), :]
-        both = part.reshape(QUAD * PIECE, 2 * DIM)
-        lanes = pl.ds(pl.multiple_of(quad * QUAD * PIECE, QUAD * PIECE), QUAD * PIECE)
+    def gathered(piece, batch):
+        sources = KEYS // SIZES[piece]
+        part = kv[pl.ds(sources * batch, sources), pl.ds(HEAD_ROWS + STARTS[piece], SIZES[piece]), :]
+        both = part.reshape(KEYS, 2 * DIM)
+        lanes = pl.ds(pl.multiple_of(CTX * STARTS[piece] + batch * KEYS, KEYS), KEYS)
         return both[:, :DIM].astype(F32).T, both[:, DIM:], lanes
 
     def moments(piece):
-        def one(quad):
-            key_t, value, lanes = gathered(piece, quad)
+        def one(batch):
+            key_t, value, lanes = gathered(piece, batch)
             double = twice(value, 0)
             for head in range(HEADS):
-                mom[head] += nn(wide(key_t * wts[0, piece, head : head + 1, lanes]), double)
-
-        each(CTX // QUAD, one)
+                mom[head] += nn(wide(key_t * wts[0, head : head + 1, lanes]), double)
+
+        each(CTX * SIZES[piece] // KEYS, one)
 
     def tangents(piece):
-        def one(quad):
-            key_t, value, lanes = gathered(piece, quad)
+        def one(batch):
+            key_t, value, lanes = gathered(piece, batch)
             for head in range(HEADS):
-                by_decay = (key_t * wts[1, piece, head : head + 1, lanes]).astype(BF16)
-                by_bias = (key_t * wts[2, piece, head : head + 1, lanes]).astype(BF16)
+                by_decay = (key_t * wts[1, head : head + 1, lanes]).astype(BF16)
+                by_bias = (key_t * wts[2, head : head + 1, lanes]).astype(BF16)
                 tangent[head] += nn(jnp.concatenate([by_decay, by_bias], axis=0), value)
 
-        each(CTX // QUAD, one)
+        each(CTX * SIZES[piece] // KEYS, one)
 
     def sort(piece):
         def one(index):
-            block = piece * (CTX // PIECES) + index
+            block = STARTS[piece] // SUB + index
             part = pl.ds(pl.multiple_of(HEAD_ROWS + SUB * block, SUB), SUB)
             both = kv[:, part, :].reshape(ROWS, 2 * DIM)
             kpos[block] = both[:, :DIM]
             vpos[block, :, :DIM] = both[:, DIM:]
             vpos[block, :, DIM:] = jnp.ones((ROWS, DIM), BF16)
 
-        each(CTX // PIECES, one)
+        each(SIZES[piece] // SUB, one)
 
     def attend(chunk, masked):
         blocks = pl.ds(WIDTH * chunk, WIDTH)
@@ -343,21 +346,30 @@
 
     def teach(chunk, carry):
         attend(chunk, False)
-        for piece in range(1, PIECES):
-
-            @pl.when(needs(chip, piece) & (chunk == STEPS * piece - 2))
-            def _(piece=piece):
-                relay(piece)
-
-            @pl.when(needs(chip, piece) & (chunk == STEPS * piece - 1))
-            def _(piece=piece):
-                arrived(piece)
-                sort(piece)
-                moments(piece)
+
+        @pl.when(needs(chip, 1) & (chunk == 0))
+        def _():
+            relay(1)
+            tangents(0)
+            arrived(1)
+            sort(1)
+
+        @pl.when(needs(chip, 2) & (chunk == 1))
+        def _():
+            relay(2)
+            moments(1)
+            arrived(2)
+            sort(2)
+            moments(2)
 
         return carry
 
     lax.fori_loop(0, last, teach, 0)
+
+    @pl.when(needs(chip, 1) & jnp.logical_not(needs(chip, 2)))
+    def _():
+        moments(1)
+
     attend(last, True)
 
     def close(head):
@@ -372,7 +384,7 @@
     vown[...] = twice(own_kv[:, DIM:], 1)
 
     def forward(group):
-        heads = [GROUP * group + index for index in range(GROUP)]
+        heads = [FORWARD * group + index for index in range(FORWARD)]
         read = [halves(nn(qh[h], both_maps[h])) for h in heads]
         score = [nt(wide(r), kown[...]) for r in read]
         causal = place(iota((ROWS, ROWS), 1)) <= place(iota((ROWS, ROWS), 0))
@@ -397,22 +409,21 @@
             stats[2] += scaled * scaled
             stats[3] += scaled * taught
 
-    each(HEADS // GROUP, forward)
-
-    lane = iota((ROWS, DIM), 1)
-    packed = jnp.zeros((ROWS, DIM), F32)
+    each(HEADS // FORWARD, forward)
+
+    line = iota((8, ROWS), 0)
+    packed = jnp.zeros((8, ROWS), F32)
     for index in range(4):
-        packed = jnp.where(lane == index, jnp.sum(stats[index], axis=1, keepdims=True), packed)
-    stx[tp] = packed.T[:8]
+        packed = jnp.where(line == index, nt(jnp.ones((8, 2 * DIM), BF16), wide(stats[index])), packed)
+    stx[tp] = packed
 
     def t_copy(peer, slot):
         return remote(stx.at[slot], stx.at[slot], t_ss.at[peer], t_rs.at[slot], {"tp": peer})
 
     others(TP, tp, lambda peer: t_copy(peer, tp).start())
-    tangents(0)
-    for piece in range(1, PIECES):
-
-        @pl.when(needs(chip, piece))
+    for piece in range(PIECES):
+
+        @pl.when(jnp.logical_not(needs(chip, 1)) if piece == 0 else needs(chip, piece))
         def _(piece=piece):
             tangents(piece)
 
@@ -453,7 +464,11 @@
         sib_copy(group).wait_recv()
         for index, head in enumerate(turns(group)):
             turn = GROUP * group + index
-            pairsum[turn] = gbuf[core, turn] + sibr[turn]
+            both = gbuf[core, turn] + sibr[turn]
+            pairsum[turn, :DIM] = both[:DIM].astype(BF16)
+            high, low = split(both[DIM:])
+            ends = jnp.concatenate([high.astype(F32), low.astype(F32)], axis=0)
+            pairsum[turn, DIM:] = ends.astype(BF16)
 
             @pl.when(head != chip)
             def _(head=head, turn=turn):
@@ -521,7 +536,9 @@
     pass_on(HEADS // GROUP - 1)
 
     others(CHIPS, chip, lambda peer: r_copy(0, peer, peer).wait_recv())
-    fin[core, order_of(chip)] = jnp.sum(rs[...], axis=0)
+    whole = jnp.sum(rs[...].astype(F32), axis=0)
+    fin[core, order_of(chip), :DIM] = whole[:DIM]
+    fin[core, order_of(chip), DIM:] = whole[DIM : DIM + TAIL] + whole[DIM + TAIL :]
 
     def ag_copy(peer, slot):
         held = fin.at[core, order_of(slot)]
@@ -536,6 +553,23 @@
         return pltpu.make_async_copy(fin.at[:, part], fin_to.at[:, part], fin_sem.at[half])
 
     others(CHIPS, chip, lambda peer: ag_copy(peer, chip).start())
+
+    others(CTX, me, lambda peer: q_copy(peer, me).wait_send())
+    for piece in range(PIECES):
+
+        def left(peer, piece=piece):
+            @pl.when(needs(peer, piece))
+            def _():
+                kv_copy(peer, chip, piece).wait_send()
+
+        others(CHIPS, chip, left)
+
+        @pl.when(needs(chip, piece))
+        def _(piece=piece):
+            for slot in range(CHIPS):
+                kf_copy(slot, core, piece).wait_send()
+
+    others(TP, tp, lambda peer: t_copy(peer, tp).wait_send())
     for half in range(2):
         for head in ORDER[half * (CHIPS // 2) : (half + 1) * (CHIPS // 2)]:
 
@@ -548,22 +582,6 @@
         fw_copy(half, 1 - core).wait_recv()
         fin_copy(half).start()
 
-    others(CTX, me, lambda peer: q_copy(peer, me).wait_send())
-    for piece in range(PIECES):
-
-        def left(peer, piece=piece):
-            @pl.when(needs(peer, piece))
-            def _():
-                kv_copy(peer, chip, piece).wait_send()
-
-        others(CHIPS, chip, left)
-
-        @pl.when(needs(chip, piece))
-        def _(piece=piece):
-            for slot in range(CHIPS):
-                kf_copy(slot, core, piece).wait_send()
-
-    others(TP, tp, lambda peer: t_copy(peer, tp).wait_send())
     others(CHIPS, chip, lambda peer: r_copy(0, peer, chip).wait_send())
     others(CHIPS, chip, lambda peer: ag_copy(peer, chip).wait_send())
     for group in range(HEADS // GROUP):
@@ -602,6 +620,7 @@
     square = (HEADS, DIM, DIM)
     by_row = (HEADS, ROWS, DIM)
     message = (DIM + TAIL, DIM)
+    short = (DIM + 2 * TAIL, DIM)
     arguments = (
         queries, keys, values, dt_logits.T, decay_log, dt_bias, c_weight, b_weight, x_weight, norm_gain,
     )
@@ -626,7 +645,7 @@
             bf16(*by_row),
             f32(*square),
             f32(HEADS, 2 * DIM, DIM),
-            f32(3, PIECES, HEADS, CTX * PIECE),
+            f32(3, HEADS, CTX * ROWS),
             f32(4, HEADS, ROWS),
             f32(*by_row),
             f32(*by_row),
@@ -648,8 +667,8 @@
             bf16(ROWS, HEADS * DIM),
             f32(2, HEADS, *message),
             f32(HEADS, *message),
-            f32(HEADS, *message),
-            f32(CHIPS, *message),
+            bf16(HEADS, *short),
+            bf16(CHIPS, *short),
             f32(2, HEADS, *message),
             bf16(HEADS, ROWS),
             pltpu.SMEM((HEADS,), F32),

time: 77.6 us -> 73 us (0.941)
  Pallas kernels: 76.6 us -> 72 us
    pallas_call x1, Pallas kernels: 74.9 us -> 70.3 us  [local(): pl.pallas_call(kernel, out_shape=(jax.ShapeDtypeStruct((ROWS, HEADS * DIM...]
where the time goes in v4:
time: 73 us; the launch traced here: 72.9 us
  Pallas kernels  72 us (99%)
  between operations  0.84 us (1%)
    pallas_call x1, Pallas kernels, local(): pl.pallas_call(kernel, out_shape=(jax.ShapeDtypeStruct((ROWS, HEADS * DIM...  70.3 us
    pallas_call x1, Pallas kernels, local(): pl.pallas_call(closing, out_shape=(jax.ShapeDtypeStruct((ROWS, HEADS * DI...  1.76 us

profile of v4, /device:TPU:1, one launch (start us, length us, event | category | flops | bytes accessed | tf_op | source)
XLA Modules:
  0.0 72.9 jit_solution(14216931640757711217)
XLA Ops:
  0.6 0.0 copy-start.1
  0.6 0.0 copy-start
  0.7 70.3 %shard_map.153 = (bf16[256,1024]{1,0:T(8,128)(2,1)S(1)}, f32[2,8,136,128]{3,2,1,0:T(8,128)S(1)}) custom-call(bf16[256,1024]{1,0:T(8,128)(2,1)} %q_in.1, bf16[256,128]{1,0:T(8,128)(2,1)} %k_in.1, bf16[256,128]{1,0:T(8,128)(2,1)} %v_in.1, bf16[8,256]{1,0:T(8,128)(2,1)} %bitcast.1, f32[8]{0:T(128)} %decay_hbm.1, f32[8]{0:T(128)} %bias_hbm.1, ...), custom_call_target="tpu_custom_call" | custom-call | tf_op jit(solution)/shard_map/pallas_call | solution.py:628
  70.9 0.0 copy-done.1
  70.9 0.0 copy-done
  70.9 1.8 %shard_map.154 = (bf16[256,1024]{1,0:T(8,128)(2,1)}, f32[8,128,128]{2,1,0:T(8,128)}, f32[8,128,128]{2,1,0:T(8,128)}, f32[8,128,128]{2,1,0:T(8,128)}, f32[8]{0:T(128)}, /*index=5*/f32[8]{0:T(128)}, f32[1024]{0:T(1024)}) custom-call(bf16[256,1024]{1,0:T(8,128)(2,1)S(1)} %get-tuple-element.9.out_in, f32[2,8,136,128]{3,2,1,0:T(8,128)S(1)} %get-tuple-element.10.fin, ...), custom_call_target="tpu_custom_call" | custom-call | tf_op jit(solution)/shard_map/pallas_call | solution.py:688
Async XLA Ops:
  0.6 70.3 %copy-start.1 = (bf16[8,128,128]{2,1,0:T(8,128)(2,1)S(1)}, bf16[8,128,128]{2,1,0:T(8,128)(2,1)}, u32[]{:S(2)}) copy-start(bf16[8,128,128]{2,1,0:T(8,128)(2,1)} %b_w.1) | copy-start | bytes 786436
  0.6 70.3 %copy-start = (bf16[8,128,128]{2,1,0:T(8,128)(2,1)S(1)}, bf16[8,128,128]{2,1,0:T(8,128)(2,1)}, u32[]{:S(2)}) copy-start(bf16[8,128,128]{2,1,0:T(8,128)(2,1)} %c_w.1) | copy-start | bytes 786436

commit v5 on v4

--- a/solution.py
+++ b/solution.py
@@ -20,6 +20,7 @@
 PIECES = len(STARTS)
 WIDTH = 4
 KEYS = 512
+STACK = 4
 HEAD_ROWS = 16
 TAIL = 8
 GROUP = 2
@@ -72,6 +73,12 @@
     return halves(nn(a_high, jnp.concatenate([b_high, b_low], axis=1))) + nn(a_low, b_high)
 
 
+def left_product(parts, b):
+    b_high, b_low = split(b)
+    high, low = parts[:, :ROWS], parts[:, ROWS:]
+    return halves(nn(high, jnp.concatenate([b_high, b_low], axis=1))) + nn(low, b_high)
+
+
 def product_t(a, b):
     a_high, a_low = split(a)
     b_high, b_low = split(b)
@@ -101,7 +108,7 @@
 def kernel(
     q_in, k_in, v_in, z_hbm, decay_hbm, bias_hbm, c_in, b_in, x_in, gain_hbm,
     out_to, fin_to,
-    qr, kv, kpos, vpos, qh, hide, acc, top, tq, mom, tangent, wts, rows, rcol, rbcol, kown, vown, gains, both_maps,
+    qr, kv, kpos, vpos, qh, hide, acc, top, tq, mom, tangent, wts, rows, rcol, rbcol, kown, vown, gains, both_maps, faded, zt_all, tt_all, qt_all,
     c_w, b_w, x_w, t_all, s_all, d_all, z_all, y_all, stats, stx, cols, out,
     gbuf, sibr, pairsum, rs, fin,
     z_in, decay_in, bias_in, gain_in,
@@ -165,6 +172,7 @@
         gains[head : head + 1, :] = gain_in[head * DIM : (head + 1) * DIM].reshape(1, DIM)
         acc[head] = jnp.zeros((ROWS, 2 * DIM), F32)
         top[head] = jnp.full((ROWS, DIM), NEG, F32)
+    vpos[:, :, DIM:] = jnp.ones((CTX, ROWS, DIM), BF16)
     mom[...] = jnp.zeros_like(mom)
     tangent[...] = jnp.zeros_like(tangent)
     stats[...] = jnp.zeros_like(stats)
@@ -286,19 +294,25 @@
     def moments(piece):
         def one(batch):
             key_t, value, lanes = gathered(piece, batch)
-            double = twice(value, 0)
-            for head in range(HEADS):
-                mom[head] += nn(wide(key_t * wts[0, head : head + 1, lanes]), double)
+            for first in range(0, HEADS, STACK):
+                parts = []
+                for head in range(first, first + STACK):
+                    parts.extend(split(key_t * wts[0, head : head + 1, lanes]))
+                added = nn(jnp.concatenate(parts, axis=0), value).reshape(STACK, 2, DIM, DIM)
+                mom[first : first + STACK] += added[:, 0] + added[:, 1]
 
         each(CTX * SIZES[piece] // KEYS, one)
 
     def tangents(piece):
         def one(batch):
             key_t, value, lanes = gathered(piece, batch)
-            for head in range(HEADS):
-                by_decay = (key_t * wts[1, head : head + 1, lanes]).astype(BF16)
-                by_bias = (key_t * wts[2, head : head + 1, lanes]).astype(BF16)
-                tangent[head] += nn(jnp.concatenate([by_decay, by_bias], axis=0), value)
+            for first in range(0, HEADS, STACK):
+                parts = []
+                for head in range(first, first + STACK):
+                    parts.append((key_t * wts[1, head : head + 1, lanes]).astype(BF16))
+                    parts.append((key_t * wts[2, head : head + 1, lanes]).astype(BF16))
+                added = nn(jnp.concatenate(parts, axis=0), value)
+                tangent[first : first + STACK] += added.reshape(STACK, 2 * DIM, DIM)
 
         each(CTX * SIZES[piece] // KEYS, one)
 
@@ -309,7 +323,6 @@
             both = kv[:, part, :].reshape(ROWS, 2 * DIM)
             kpos[block] = both[:, :DIM]
             vpos[block, :, :DIM] = both[:, DIM:]
-            vpos[block, :, DIM:] = jnp.ones((ROWS, DIM), BF16)
 
         each(SIZES[piece] // SUB, one)
 
@@ -397,7 +410,9 @@
             d_all[h] = decay
             high, low = split(s * decay)
             value = vown[:, :DIM]
-            mixed.append(nn(high, value) + nn(low, value) + jnp.exp(rcol[h]) * product(r, mom[h]))
+            fade = jnp.exp(rcol[h])
+            faded[h] = fade
+            mixed.append(nn(high, value) + nn(low, value) + fade * product(r, mom[h]))
         flats = [nn(wide(m), twice(x_w[h], 0)) for h, m in zip(heads, mixed)]
         for h, m, flat in zip(heads, mixed, flats):
             z_all[h] = m
@@ -427,6 +442,12 @@
         def _(piece=piece):
             tangents(piece)
 
+    def turn_over(head):
+        zt_all[head] = wide(z_all[head].T)
+        tt_all[head] = wide(t_all[head].T)
+        qt_all[head] = qh[head].astype(F32).T.astype(BF16)
+
+    each(HEADS, turn_over)
     others(TP, tp, lambda peer: t_copy(peer, peer).wait_recv())
     sums = jnp.sum(stx[...], axis=0)
     inverse = lax.rsqrt(sums[0:1] / FEATURES + EPS)
@@ -481,14 +502,12 @@
     def backward(group):
         heads = turns(group)
         d_flats, small = [], []
-        order = jnp.where(iota((ROWS, ROWS), 0) == place(iota((ROWS, ROWS), 1)), 1.0, 0.0).astype(BF16)
         for h in heads:
             flat = y_all[h]
             gain = gains[pl.ds(h, 1), :]
             inv = cols[0]
             unit = flat * inv
             normed = unit * gain
-            out[:, pl.ds(pl.multiple_of(h * DIM, DIM), DIM)] = nn(order, normed.astype(BF16)).astype(BF16)
             d_normed = (2.0 / TOKENS) * (normed - tq[h].astype(F32) * cols[1])
             d_flat = d_normed * gain * inv - flat * cols[2]
             d_flats.append(d_flat)
@@ -501,7 +520,7 @@
         d_mixed = [nt(wide(d), twice(x_w[h], 1)) for h, d in zip(heads, d_flats)]
         d_score = [nt(wide(d), vown[...]) * d_all[h] for h, d in zip(heads, d_mixed)]
         for index, h in enumerate(heads):
-            gbuf[1, GROUP * group + index, :DIM] = product(z_all[h].T, d_flats[index])
+            gbuf[1, GROUP * group + index, :DIM] = left_product(zt_all[h], d_flats[index])
         d_read = []
         for index, h in enumerate(heads):
             felt = jnp.sum(d_score[index] * s_all[h], axis=0, keepdims=True)
@@ -509,16 +528,15 @@
             from_bias = felt * (rows[3, pl.ds(h, 1), :] - rows[2, pl.ds(h, 1), :])
             high, low = split(d_score[index])
             key = kown[:, :DIM]
-            d_late = jnp.exp(rcol[h]) * d_mixed[index]
+            d_late = faded[h] * d_mixed[index]
             d_read.append(nn(high, key) + nn(low, key) + product_t(d_late, mom[h]))
-            d_state = product(t_all[h].T, d_late)
+            d_state = left_product(tt_all[h], d_late)
             small[index][1] += jnp.sum(d_state * tangent[h, :DIM], axis=0, keepdims=True) - halves(from_decay)
             small[index][2] += jnp.sum(d_state * tangent[h, DIM:], axis=0, keepdims=True) + halves(from_bias)
         tail = iota((TAIL, DIM), 0)
         for index, h in enumerate(heads):
-            query_t = qh[h].astype(F32).T.astype(BF16)
             turn = GROUP * group + index
-            gbuf[0, turn, :DIM] = halves(nn(query_t, wide(d_read[index])))
+            gbuf[0, turn, :DIM] = halves(nn(qt_all[h], wide(d_read[index])))
             lines = jnp.zeros((TAIL, DIM), F32)
             for line, value in enumerate(small[index]):
                 lines = jnp.where(tail == line, value, lines)
@@ -531,8 +549,6 @@
             pass_on(group - 1)
 
     each(HEADS // GROUP, backward)
-    out_copy = pltpu.make_async_copy(out, out_to, out_sem.at[0])
-    out_copy.start()
     pass_on(HEADS // GROUP - 1)
 
     others(CHIPS, chip, lambda peer: r_copy(0, peer, peer).wait_recv())
@@ -553,6 +569,13 @@
         return pltpu.make_async_copy(fin.at[:, part], fin_to.at[:, part], fin_sem.at[half])
 
     others(CHIPS, chip, lambda peer: ag_copy(peer, chip).start())
+
+    order = jnp.where(iota((ROWS, ROWS), 0) == place(iota((ROWS, ROWS), 1)), 1.0, 0.0).astype(BF16)
+    for head in range(HEADS):
+        normed = y_all[head] * cols[0] * gains[head : head + 1, :]
+        out[:, head * DIM : (head + 1) * DIM] = nn(order, normed.astype(BF16)).astype(BF16)
+    out_copy = pltpu.make_async_copy(out, out_to, out_sem.at[0])
+    out_copy.start()
 
     others(CTX, me, lambda peer: q_copy(peer, me).wait_send())
     for piece in range(PIECES):
@@ -653,6 +676,10 @@
             bf16(ROWS, 2 * DIM),
             f32(HEADS, DIM),
             bf16(HEADS, DIM, 2 * DIM),
+            f32(*by_row),
+            bf16(HEADS, DIM, 2 * ROWS),
+            bf16(HEADS, DIM, 2 * ROWS),
+            bf16(HEADS, DIM, ROWS),
             bf16(*square),
             bf16(*square),
             bf16(*square),

time: 73 us -> 72.9 us (level)
  no operation moved by 1% of the time
where the time goes in v5:
time: 72.9 us; the launch traced here: 72.7 us
  Pallas kernels  71.9 us (99%)
  between operations  0.84 us (1%)
    pallas_call x1, Pallas kernels, local(): pl.pallas_call(kernel, out_shape=(jax.ShapeDtypeStruct((ROWS, HEADS * DIM...  70.1 us
    pallas_call x1, Pallas kernels, local(): pl.pallas_call(closing, out_shape=(jax.ShapeDtypeStruct((ROWS, HEADS * DI...  1.76 us

profile of v5, /device:TPU:1, one launch (start us, length us, event | category | flops | bytes accessed | tf_op | source)
XLA Modules:
  0.0 72.7 jit_solution(5509011212895724977)
XLA Ops:
  0.6 0.0 copy-start.1
  0.6 0.0 copy-start
  0.7 70.1 %shard_map.153 = (bf16[256,1024]{1,0:T(8,128)(2,1)S(1)}, f32[2,8,136,128]{3,2,1,0:T(8,128)S(1)}) custom-call(bf16[256,1024]{1,0:T(8,128)(2,1)} %q_in.1, bf16[256,128]{1,0:T(8,128)(2,1)} %k_in.1, bf16[256,128]{1,0:T(8,128)(2,1)} %v_in.1, bf16[8,256]{1,0:T(8,128)(2,1)} %bitcast.1, f32[8]{0:T(128)} %decay_hbm.1, f32[8]{0:T(128)} %bias_hbm.1, ...), custom_call_target="tpu_custom_call" | custom-call | tf_op jit(solution)/shard_map/pallas_call | solution.py:651
  70.8 0.0 copy-done.1
  70.8 0.0 copy-done
  70.8 1.8 %shard_map.154 = (bf16[256,1024]{1,0:T(8,128)(2,1)}, f32[8,128,128]{2,1,0:T(8,128)}, f32[8,128,128]{2,1,0:T(8,128)}, f32[8,128,128]{2,1,0:T(8,128)}, f32[8]{0:T(128)}, /*index=5*/f32[8]{0:T(128)}, f32[1024]{0:T(1024)}) custom-call(bf16[256,1024]{1,0:T(8,128)(2,1)S(1)} %get-tuple-element.9.out_in, f32[2,8,136,128]{3,2,1,0:T(8,128)S(1)} %get-tuple-element.10.fin, ...), custom_call_target="tpu_custom_call" | custom-call | tf_op jit(solution)/shard_map/pallas_call | solution.py:715
Async XLA Ops:
  0.6 70.2 %copy-start.1 = (bf16[8,128,128]{2,1,0:T(8,128)(2,1)S(1)}, bf16[8,128,128]{2,1,0:T(8,128)(2,1)}, u32[]{:S(2)}) copy-start(bf16[8,128,128]{2,1,0:T(8,128)(2,1)} %b_w.1) | copy-start | bytes 786436
  0.6 70.2 %copy-start = (bf16[8,128,128]{2,1,0:T(8,128)(2,1)S(1)}, bf16[8,128,128]{2,1,0:T(8,128)(2,1)}, u32[]{:S(2)}) copy-start(bf16[8,128,128]{2,1,0:T(8,128)(2,1)} %c_w.1) | copy-start | bytes 786436
